TPU v7x, 32 devices: a whole 2x2x4 slice. The times are simulated.
32 devices in a mesh: dp: 16 (over z, y, x), tensor: 2 (over core).
Axes of the slice: x: 2, y: 2, z: 4, core: 2. Of those that a mesh axis runs over, the one named last changes fastest.
Arguments:
- layer_in: bfloat16 [4096, 768], P(('dp', 'tensor')), may hold values from -6 to 6
- enc_states: bfloat16 [2048, 768], P(('dp', 'tensor')), may hold values from -6 to 6
- cotangent: bfloat16 [4096, 768], P(('dp', 'tensor')), may hold values from -6 to 6
- gain_self: float32 [768], replicated, may hold values from 0.25 to 1.75
- gain_cross: float32 [768], replicated, may hold values from 0.25 to 1.75
- gain_feed: float32 [768], replicated, may hold values from 0.25 to 1.75
- bias_table: float32 [32, 12], replicated, may hold values from -5 to 5
- self_query: bfloat16 [768, 768], P('dp', 'tensor'), may hold values from -0.0546875 to 0.0546875
- self_key: bfloat16 [768, 768], P('dp', 'tensor'), may hold values from -0.21875 to 0.21875
- self_value: bfloat16 [768, 768], P('dp', 'tensor'), may hold values from -0.21875 to 0.21875
- self_out: bfloat16 [768, 768], P('tensor', 'dp'), may hold values from -0.4375 to 0.4375
- cross_query: bfloat16 [768, 768], P('dp', 'tensor'), may hold values from -0.0546875 to 0.0546875
- cross_key: bfloat16 [768, 768], P('dp', 'tensor'), may hold values from -0.21875 to 0.21875
- cross_value: bfloat16 [768, 768], P('dp', 'tensor'), may hold values from -0.21875 to 0.21875
- cross_out: bfloat16 [768, 768], P('tensor', 'dp'), may hold values from -0.4375 to 0.4375
- gate_proj: bfloat16 [768, 2048], P('dp', 'tensor'), may hold values from -0.21875 to 0.21875
- up_proj: bfloat16 [768, 2048], P('dp', 'tensor'), may hold values from -0.21875 to 0.21875
- down_proj: bfloat16 [2048, 768], P('tensor', 'dp'), may hold values from -0.25 to 0.25
- dec_lengths: int32 [16], replicated, may hold values from 1 to 256, 3276 in all
- enc_lengths: int32 [16], replicated, may hold values from 1 to 128, 1280 in all
- seq_owner: int32 [16], replicated, may hold values from 0 to 15, each once
- bucket_table: int32 [256], replicated, may hold values from 0 to 31
Outputs:
- layer_out: bfloat16 [4096, 768], P(('dp', 'tensor'))
- grad_in: float32 [4096, 768], P(('dp', 'tensor'))
- grad_states: float32 [2048, 768], P(('dp', 'tensor'))
- grad_gain_self: float32 [768], replicated
- grad_gain_cross: float32 [768], replicated
- grad_gain_feed: float32 [768], replicated
- grad_table: float32 [32, 12], replicated
- grad_self_query: float32 [768, 768], P('dp', 'tensor')
- grad_self_key: float32 [768, 768], P('dp', 'tensor')
- grad_self_value: float32 [768, 768], P('dp', 'tensor')
- grad_self_out: float32 [768, 768], P('tensor', 'dp')
- grad_cross_query: float32 [768, 768], P('dp', 'tensor')
- grad_cross_key: float32 [768, 768], P('dp', 'tensor')
- grad_cross_value: float32 [768, 768], P('dp', 'tensor')
- grad_cross_out: float32 [768, 768], P('tensor', 'dp')
- grad_gate_proj: float32 [768, 2048], P('dp', 'tensor')
- grad_up_proj: float32 [768, 2048], P('dp', 'tensor')
- grad_down_proj: float32 [2048, 768], P('tensor', 'dp')
Inputs may be any that keep to these rules, and one draw needn't show every extreme that they name: `dec_lengths`: one sequence has exactly 256 decoder tokens. `enc_lengths`: one sequence has exactly 128 encoder tokens. `seq_owner`: each sequence in exactly one slot.
All inputs are finite; a program needn't handle non-finite values.
Results may differ from a plain program's by a relative error of at most 0.039.
Values may be sent and summed in bfloat16 or wider, within the bound.
No kernel may reach another device: no remote copies, remote signals or barrier semaphores. Data moves between devices by JAX's collectives and lax.ppermute only.
A program may use at most 192 MiB of HBM per device.

v0:
```python
import jax
import jax.numpy as jnp
from jax import lax
from jax.sharding import PartitionSpec as P

H = 12
DH = 64
NB = 32
LEN = 256
ENC = 128


EPSILON = 1e-06
NEGATIVE = -1e30


def norm_rows(values, gain):
    return values * lax.rsqrt(jnp.mean(values * values, axis=-1, keepdims=True) + EPSILON) * gain


def norm_back(values, gain, upstream):
    result, pull = jax.vjp(norm_rows, values, gain)
    return pull(upstream)


def whole_rows(block):
    return lax.all_gather(block, "tensor", axis=0, tiled=True)


def split_rows(terms):
    return lax.psum_scatter(
        terms.astype(jnp.bfloat16), "tensor", scatter_dimension=0, tiled=True
    ).astype(jnp.float32)


def product(left, right):
    return jnp.dot(left, right, preferred_element_type=jnp.float32)


def product_tn(left, right):
    return lax.dot_general(
        left, right, (((0,), (0,)), ((), ())), preferred_element_type=jnp.float32
    )


def product_nt(left, right):
    return lax.dot_general(
        left, right, (((1,), (1,)), ((), ())), preferred_element_type=jnp.float32
    )


def split_heads(matrix):
    return matrix.reshape(matrix.shape[0], -1, DH)


def scores_of(query, keys, extra, allowed):
    raw = jnp.einsum("qhd,khd->hqk", query, keys, preferred_element_type=jnp.float32) + extra
    return jnp.where(allowed, raw, NEGATIVE)


def attend_forward(query, keys, values, extra, allowed):
    scores = scores_of(query, keys, extra, allowed)
    highest = jnp.max(scores, axis=-1, keepdims=True)
    expo = jnp.exp(scores - highest)
    total = jnp.sum(expo, axis=-1, keepdims=True)
    probs = expo / total
    mixed = jnp.einsum(
        "hqk,khd->qhd", probs.astype(jnp.bfloat16), values, preferred_element_type=jnp.float32
    ).astype(jnp.bfloat16)
    return (mixed.reshape(mixed.shape[0], -1), highest + jnp.log(total))


def attend_backward(query, keys, values, extra, allowed, log_total, grad_mixed):
    probs = jnp.exp(scores_of(query, keys, extra, allowed) - log_total)
    upstream = split_heads(grad_mixed)
    grad_probs = jnp.einsum("qhd,khd->hqk", upstream, values, preferred_element_type=jnp.float32)
    inner = jnp.sum(probs * grad_probs, axis=-1, keepdims=True)
    grad_scores = (probs * (grad_probs - inner)).astype(jnp.bfloat16)
    grad_query = jnp.einsum("hqk,khd->qhd", grad_scores, keys, preferred_element_type=jnp.float32)
    grad_keys = jnp.einsum("hqk,qhd->khd", grad_scores, query, preferred_element_type=jnp.float32)
    grad_values = jnp.einsum(
        "hqk,qhd->khd", probs.astype(jnp.bfloat16), upstream, preferred_element_type=jnp.float32
    )
    rows_q = grad_query.shape[0]
    rows_k = grad_keys.shape[0]
    return (
        grad_query.reshape(rows_q, -1).astype(jnp.bfloat16),
        grad_keys.reshape(rows_k, -1).astype(jnp.bfloat16),
        grad_values.reshape(rows_k, -1).astype(jnp.bfloat16),
        grad_scores,
    )


def shards(
    layer_in,
    enc_states,
    cotangent,
    gain_self,
    gain_cross,
    gain_feed,
    bias_table,
    self_query,
    self_key,
    self_value,
    self_out,
    cross_query,
    cross_key,
    cross_value,
    cross_out,
    gate_proj,
    up_proj,
    down_proj,
    dec_lengths,
    enc_lengths,
    seq_owner,
    bucket_table,
):
    weights = (
        lax.all_gather(self_query, "dp", axis=0, tiled=True),
        lax.all_gather(self_key, "dp", axis=0, tiled=True),
        lax.all_gather(self_value, "dp", axis=0, tiled=True),
        lax.all_gather(self_out, "dp", axis=1, tiled=True),
        lax.all_gather(cross_query, "dp", axis=0, tiled=True),
        lax.all_gather(cross_key, "dp", axis=0, tiled=True),
        lax.all_gather(cross_value, "dp", axis=0, tiled=True),
        lax.all_gather(cross_out, "dp", axis=1, tiled=True),
        lax.all_gather(gate_proj, "dp", axis=0, tiled=True),
        lax.all_gather(up_proj, "dp", axis=0, tiled=True),
        lax.all_gather(down_proj, "dp", axis=1, tiled=True),
    )
    w_query, w_key, w_value, w_out, c_query, c_key, c_value, c_out, w_gate, w_up, w_down = weights
    owner = seq_owner[lax.axis_index("dp")]
    length = dec_lengths[owner]
    enc_len = enc_lengths[owner]
    half_rows = layer_in.shape[0]
    row_pos = lax.axis_index("tensor") * half_rows + jnp.arange(half_rows)
    valid = (row_pos < length).astype(jnp.float32)[:, None]
    position = jnp.arange(LEN)
    causal = ((position[None, :] <= position[:, None]) & (position[None, :] < length))[None]
    allowed = (jnp.arange(ENC) < enc_len)[None, None, :]
    local_heads = w_query.shape[1] // DH
    head_start = lax.axis_index("tensor") * local_heads
    table_part = lax.dynamic_slice_in_dim(bias_table, head_start, local_heads, 1)
    distance = jnp.clip(position[:, None] - position[None, :], 0, LEN - 1)
    onehot = (bucket_table[:, None] == jnp.arange(NB)[None, :]).astype(jnp.float32)

    def build_extra(part):
        per_dist = jnp.dot(onehot, part, precision=lax.Precision.HIGHEST)
        return jnp.transpose(per_dist[distance], (2, 0, 1))

    extra, extra_pull = jax.vjp(build_extra, table_part)
    inputs = layer_in.astype(jnp.float32)
    whole_self = whole_rows(norm_rows(inputs, gain_self).astype(jnp.bfloat16))
    query = product(whole_self, w_query).astype(jnp.bfloat16)
    keys = product(whole_self, w_key).astype(jnp.bfloat16)
    values = product(whole_self, w_value).astype(jnp.bfloat16)
    mixed_self, total_self_fwd = attend_forward(
        split_heads(query), split_heads(keys), split_heads(values), extra, causal
    )
    after_self = inputs + split_rows(product(mixed_self, w_out))
    whole_cross = whole_rows(norm_rows(after_self, gain_cross).astype(jnp.bfloat16))
    whole_states = whole_rows(enc_states)
    cross_q = product(whole_cross, c_query).astype(jnp.bfloat16)
    cross_k = product(whole_states, c_key).astype(jnp.bfloat16)
    cross_v = product(whole_states, c_value).astype(jnp.bfloat16)
    mixed_cross, total_cross_fwd = attend_forward(
        split_heads(cross_q), split_heads(cross_k), split_heads(cross_v), 0.0, allowed
    )
    after_cross = after_self + split_rows(product(mixed_cross, c_out))
    whole_feed = whole_rows(norm_rows(after_cross, gain_feed).astype(jnp.bfloat16))
    gate = product(whole_feed, w_gate)
    upper = product(whole_feed, w_up)

    def geglu(gate_in, upper_in):
        return jax.nn.gelu(gate_in, approximate=True) * upper_in

    activated, geglu_pull = jax.vjp(geglu, gate, upper)
    hidden = activated.astype(jnp.bfloat16)
    layer_out = (after_cross + split_rows(product(hidden, w_down))).astype(jnp.bfloat16)
    weights = (
        lax.all_gather(self_query, "dp", axis=0, tiled=True),
        lax.all_gather(self_key, "dp", axis=0, tiled=True),
        lax.all_gather(self_value, "dp", axis=0, tiled=True),
        lax.all_gather(self_out, "dp", axis=1, tiled=True),
        lax.all_gather(cross_query, "dp", axis=0, tiled=True),
        lax.all_gather(cross_key, "dp", axis=0, tiled=True),
        lax.all_gather(cross_value, "dp", axis=0, tiled=True),
        lax.all_gather(cross_out, "dp", axis=1, tiled=True),
        lax.all_gather(gate_proj, "dp", axis=0, tiled=True),
        lax.all_gather(up_proj, "dp", axis=0, tiled=True),
        lax.all_gather(down_proj, "dp", axis=1, tiled=True),
    )
    w_query, w_key, w_value, w_out, c_query, c_key, c_value, c_out, w_gate, w_up, w_down = weights
    top = cotangent.astype(jnp.float32) * valid
    whole_top = whole_rows(top.astype(jnp.bfloat16))
    grad_hidden = product_nt(whole_top, w_down)
    grad_down = product_tn(hidden, whole_top)
    grad_gate_rows, grad_up_rows = geglu_pull(grad_hidden)
    grad_gate_rows = grad_gate_rows.astype(jnp.bfloat16)
    grad_up_rows = grad_up_rows.astype(jnp.bfloat16)
    grad_gate = product_tn(whole_feed, grad_gate_rows)
    grad_up = product_tn(whole_feed, grad_up_rows)
    grad_normed = split_rows(product_nt(grad_gate_rows, w_gate) + product_nt(grad_up_rows, w_up))
    back_feed, grad_gain_feed = norm_back(after_cross, gain_feed, grad_normed)
    total_cross = top + back_feed
    whole_grad = whole_rows(total_cross.astype(jnp.bfloat16))
    grad_mixed = product_nt(whole_grad, c_out).astype(jnp.bfloat16)
    grad_c_out = product_tn(mixed_cross, whole_grad)
    grad_cq, grad_ck, grad_cv, unused_scores = attend_backward(
        split_heads(cross_q),
        split_heads(cross_k),
        split_heads(cross_v),
        0.0,
        allowed,
        total_cross_fwd,
        grad_mixed,
    )
    grad_c_query = product_tn(whole_cross, grad_cq)
    grad_c_key = product_tn(whole_states, grad_ck)
    grad_c_value = product_tn(whole_states, grad_cv)
    grad_states = split_rows(product_nt(grad_ck, c_key) + product_nt(grad_cv, c_value))
    grad_normed = split_rows(product_nt(grad_cq, c_query))
    back_cross, grad_gain_cross = norm_back(after_self, gain_cross, grad_normed)
    total_self = total_cross + back_cross
    whole_grad = whole_rows(total_self.astype(jnp.bfloat16))
    grad_mixed = product_nt(whole_grad, w_out).astype(jnp.bfloat16)
    grad_w_out = product_tn(mixed_self, whole_grad)
    grad_q, grad_k, grad_v, grad_scores = attend_backward(
        split_heads(query),
        split_heads(keys),
        split_heads(values),
        extra,
        causal,
        total_self_fwd,
        grad_mixed,
    )
    table_grad_part = extra_pull(grad_scores.astype(jnp.float32))[0]
    table_grad = lax.dynamic_update_slice_in_dim(
        jnp.zeros((NB, H), jnp.float32), table_grad_part, head_start, 1
    )
    grad_w_query = product_tn(whole_self, grad_q)
    grad_w_key = product_tn(whole_self, grad_k)
    grad_w_value = product_tn(whole_self, grad_v)
    grad_normed = split_rows(
        product_nt(grad_q, w_query) + product_nt(grad_k, w_key) + product_nt(grad_v, w_value)
    )
    back_self, grad_gain_self = norm_back(inputs, gain_self, grad_normed)
    grad_in = total_self + back_self
    small = lax.psum(
        (grad_gain_self, grad_gain_cross, grad_gain_feed, table_grad), ("dp", "tensor")
    )
    summed = (
        lax.psum_scatter(grad_w_query, "dp", scatter_dimension=0, tiled=True),
        lax.psum_scatter(grad_w_key, "dp", scatter_dimension=0, tiled=True),
        lax.psum_scatter(grad_w_value, "dp", scatter_dimension=0, tiled=True),
        lax.psum_scatter(grad_w_out, "dp", scatter_dimension=1, tiled=True),
        lax.psum_scatter(grad_c_query, "dp", scatter_dimension=0, tiled=True),
        lax.psum_scatter(grad_c_key, "dp", scatter_dimension=0, tiled=True),
        lax.psum_scatter(grad_c_value, "dp", scatter_dimension=0, tiled=True),
        lax.psum_scatter(grad_c_out, "dp", scatter_dimension=1, tiled=True),
        lax.psum_scatter(grad_gate, "dp", scatter_dimension=0, tiled=True),
        lax.psum_scatter(grad_up, "dp", scatter_dimension=0, tiled=True),
        lax.psum_scatter(grad_down, "dp", scatter_dimension=1, tiled=True),
    )
    return (
        layer_out,
        grad_in,
        grad_states,
        small[0],
        small[1],
        small[2],
        small[3],
        summed[0],
        summed[1],
        summed[2],
        summed[3],
        summed[4],
        summed[5],
        summed[6],
        summed[7],
        summed[8],
        summed[9],
        summed[10],
    )


def solution(mesh):
    in_specs = (
        P(("dp", "tensor"), None),
        P(("dp", "tensor"), None),
        P(("dp", "tensor"), None),
        P(),
        P(),
        P(),
        P(),
        P("dp", "tensor"),
        P("dp", "tensor"),
        P("dp", "tensor"),
        P("tensor", "dp"),
        P("dp", "tensor"),
        P("dp", "tensor"),
        P("dp", "tensor"),
        P("tensor", "dp"),
        P("dp", "tensor"),
        P("dp", "tensor"),
        P("tensor", "dp"),
        P(),
        P(),
        P(),
        P(),
    )
    out_specs = (
        P(("dp", "tensor"), None),
        P(("dp", "tensor"), None),
        P(("dp", "tensor"), None),
        P(),
        P(),
        P(),
        P(),
        P("dp", "tensor"),
        P("dp", "tensor"),
        P("dp", "tensor"),
        P("tensor", "dp"),
        P("dp", "tensor"),
        P("dp", "tensor"),
        P("dp", "tensor"),
        P("tensor", "dp"),
        P("dp", "tensor"),
        P("dp", "tensor"),
        P("tensor", "dp"),
    )
    return jax.shard_map(shards, mesh=mesh, in_specs=in_specs, out_specs=out_specs, check_vma=False)
```

profile of v0, /device:TPU:0, one launch (start us, length us, event | category | flops | bytes accessed | tf_op | source)
XLA Modules:
  0.0 2296.5 jit_solution(11908473388556265056)
XLA Ops:
  8.1 1.2 dynamic_slice.12
  13.9 2.2 all_gather.65
  16.1 46.3 %all_gather.66 = bf16[768,384]{1,0:T(8,128)(2,1)S(1)} all-gather(bf16[48,384]{1,0:T(8,128)(2,1)} %param.31), channel_id=1, replica_groups=mesh['dp'=16,'tensor'=2] {'dp'}, dimensions={0}, use_global_device_ids=true | all-gather | bytes 626688 | tf_op jit(solution)/shard_map/all_gather | solution.py:121
  64.9 217.1 %gather_fusion = f32[65536,6]{1,0:T(8,128)} fusion(f32[256,6]{1,0:T(8,128)S(1)} %fusion.46, s32[65536]{0:T(1024)S(1)} %broadcast_clamp_fusion), kind=kCustom, calls=%fused_computation | custom fusion | bytes 3407872 | tf_op jit(solution)/shard_map/jvp()/gather | solution.py:149
  282.0 19.9 copy.119
  304.0 39.1 %all_gather.67 = bf16[768,384]{1,0:T(8,128)(2,1)S(1)} all-gather(bf16[48,384]{1,0:T(8,128)(2,1)S(1)} %copy-done.79), channel_id=1, replica_groups=mesh['dp'=16,'tensor'=2] {'dp'}, dimensions={0}, use_global_device_ids=true | all-gather | bytes 626688 | tf_op jit(solution)/shard_map/all_gather | solution.py:119
  344.5 41.7 %all_gather.68 = bf16[768,384]{1,0:T(8,128)(2,1)S(1)} all-gather(bf16[48,384]{1,0:T(8,128)(2,1)S(1)} %copy-done.80), channel_id=1, replica_groups=mesh['dp'=16,'tensor'=2] {'dp'}, dimensions={0}, use_global_device_ids=true | all-gather | bytes 626688 | tf_op jit(solution)/shard_map/all_gather | solution.py:120
  387.6 38.7 %all_gather.69 = bf16[384,768]{0,1:T(8,128)(2,1)S(1)} all-gather(bf16[384,48]{0,1:T(8,128)(2,1)S(1)} %copy-done.81), channel_id=1, replica_groups=mesh['dp'=16,'tensor'=2] {'dp'}, dimensions={1}, use_global_device_ids=true | all-gather | bytes 626688 | tf_op jit(solution)/shard_map/all_gather | solution.py:122
  426.3 3.3 fusion.59
  432.1 1.9 all_gather.70
  434.0 41.3 %all_gather.74 = bf16[768,384]{1,0:T(8,128)(2,1)S(1)} all-gather(bf16[48,384]{1,0:T(8,128)(2,1)S(1)} %copy-done.82), channel_id=1, replica_groups=mesh['dp'=16,'tensor'=2] {'dp'}, dimensions={0}, use_global_device_ids=true | all-gather | bytes 626688 | tf_op jit(solution)/shard_map/all_gather | solution.py:124
  475.4 38.8 %all_gather.71 = bf16[768,384]{1,0:T(8,128)(2,1)S(1)} all-gather(bf16[48,384]{1,0:T(8,128)(2,1)S(1)} %copy-done.83), channel_id=1, replica_groups=mesh['dp'=16,'tensor'=2] {'dp'}, dimensions={0}, use_global_device_ids=true | all-gather | bytes 626688 | tf_op jit(solution)/shard_map/all_gather | solution.py:125
  516.8 41.3 %all_gather.73 = bf16[768,384]{1,0:T(8,128)(2,1)S(1)} all-gather(bf16[48,384]{1,0:T(8,128)(2,1)S(1)} %copy-done.84), channel_id=1, replica_groups=mesh['dp'=16,'tensor'=2] {'dp'}, dimensions={0}, use_global_device_ids=true | all-gather | bytes 626688 | tf_op jit(solution)/shard_map/all_gather | solution.py:123
  558.1 41.6 %all_gather.75 = bf16[384,768]{0,1:T(8,128)(2,1)} all-gather(bf16[384,48]{0,1:T(8,128)(2,1)S(1)} %copy-done.85), channel_id=1, replica_groups=mesh['dp'=16,'tensor'=2] {'dp'}, dimensions={1}, use_global_device_ids=true | all-gather | bytes 626688 | tf_op jit(solution)/shard_map/all_gather | solution.py:126
  602.4 2.1 all_gather.72
  612.0 2.2 all_gather.80
  617.4 2.1 all_gather.76
  619.5 48.1 %all-gather.4.cloned.1.call-done = bf16[768,1024]{1,0:T(8,128)(2,1)} async-done(((bf16[48,1024]{1,0:T(8,128)(2,1)}), bf16[768,1024]{1,0:T(8,128)(2,1)}) %all-gather.4.cloned.1.call-update) | async-done | bytes 1572880 | tf_op jit(solution)/shard_map/all_gather | solution.py:127
  667.6 3.0 fusion.62
  670.6 56.3 %all-gather.6.cloned.1.call-done = bf16[768,1024]{1,0:T(8,128)(2,1)} async-done(((bf16[48,1024]{1,0:T(8,128)(2,1)}), bf16[768,1024]{1,0:T(8,128)(2,1)}) %all-gather.6.cloned.1.call-update) | async-done | bytes 1572880 | tf_op jit(solution)/shard_map/all_gather | solution.py:128
  727.0 3.1 fusion.63
  730.0 56.3 %all-gather.8.cloned.1.call-done = bf16[1024,768]{0,1:T(8,128)(2,1)} async-done(((bf16[1024,48]{0,1:T(8,128)(2,1)}), bf16[1024,768]{0,1:T(8,128)(2,1)}) %all-gather.8.cloned.1.call-update) | async-done | bytes 1572880 | tf_op jit(solution)/shard_map/all_gather | solution.py:129
  786.3 4.3 multiply_convert_fusion.1
  792.4 1.4 fusion.7
  794.7 5.5 reduce-scatter.29.cloned.1.call-done
  800.2 1.9 fusion.32
  802.8 1.4 fusion.56
  804.2 2.1 all_gather.81
  808.1 1.7 copy.125
  809.8 1.4 multiply_reduce_fusion.1
  815.0 2.9 convolution_convert_fusion
  818.0 1.4 convolution_convert_fusion.17
  820.0 1.4 fusion.66
  823.5 1.8 fusion.33
  825.3 1.2 multiply_multiply_fusion.4
  826.5 7.9 reduce-scatter.27.cloned.1.call-done
  834.3 2.4 fusion.57
  836.7 2.1 all_gather.82
  840.9 1.5 multiply_reduce_fusion
  848.4 1.4 fusion.71
  850.2 1.4 copy.151
  852.1 1.4 copy.153
  853.6 1.4 fusion.72
  855.1 1.4 fusion.67
  856.6 1.4 fusion.68
  858.2 1.4 fusion.69
  859.7 1.5 fusion.70
  861.3 2.4 fusion.73
  864.7 2.2 fusion.74
  868.1 2.3 fusion.75
  870.4 1.7 convert_element_type.263
  872.1 3.5 fusion.19
  875.7 17.8 copy.150
  893.5 396.3 %scatter_custom_fusion = f32[256,6]{1,0:T(8,128)S(1)} fusion(s32[65536]{0:T(1024)} %bitcast.182, f32[65536,6]{1,0:T(8,128)} %bitcast.162, f32[]{:T(128)} %constant.21.clone.1), kind=kCustom, calls=%fused_computation.117 | custom fusion | flops 393216 | bytes 6656 | tf_op jit(solution)/shard_map/transpose(jvp())/scatter-add | solution.py:149
  1291.4 41.1 %all-reduce = (f32[768]{0:T(1024)}, f32[768]{0:T(1024)}, f32[768]{0:T(1024)}, f32[32,12]{0,1:T(8,128)}) all-reduce(f32[768]{0:T(1024)S(1)} %get-tuple-element.94, f32[768]{0:T(1024)S(1)} %copy-done.89, f32[768]{0:T(1024)S(1)} %copy-done.88, f32[32,12]{0,1:T(8,128)S(1)} %dynamic_update_slice.3), channel_id=1, replica_groups=mesh['dp'=16,'tensor'=2] {'dp','tensor'}, use_global_device_ids=true, to_apply=%region_20.21 | all-reduce | flops 2688 | bytes 21504 | tf_op jit(solution)/shard_map/psum | solution.py:249
  1332.5 1.8 fusion.37
  1334.3 37.1 %reduce-scatter.47.cloned.1.call-done = f32[384,48]{0,1:T(8,128)} async-done(((f32[384,768]{0,1:T(8,128)}), f32[384,48]{0,1:T(8,128)}) %reduce-scatter.47.cloned.1.call-update) | async-done | bytes 73744 | tf_op jit(solution)/shard_map/reduce_scatter | solution.py:260
  1371.5 127.8 %reduce-scatter.37.cloned.1.call-done = f32[48,384]{1,0:T(8,128)} async-done(((f32[768,384]{1,0:T(8,128)}), f32[48,384]{1,0:T(8,128)}) %reduce-scatter.37.cloned.1.call-update) | async-done | bytes 73744 | tf_op jit(solution)/shard_map/reduce_scatter | solution.py:253
  1499.3 128.0 %reduce-scatter.39.cloned.1.call-done = f32[48,384]{1,0:T(8,128)} async-done(((f32[768,384]{1,0:T(8,128)}), f32[48,384]{1,0:T(8,128)}) %reduce-scatter.39.cloned.1.call-update) | async-done | bytes 73744 | tf_op jit(solution)/shard_map/reduce_scatter | solution.py:254
  1627.3 127.8 %reduce-scatter.41.cloned.1.call-done = f32[48,384]{1,0:T(8,128)} async-done(((f32[768,384]{1,0:T(8,128)}), f32[48,384]{1,0:T(8,128)}) %reduce-scatter.41.cloned.1.call-update) | async-done | bytes 73744 | tf_op jit(solution)/shard_map/reduce_scatter | solution.py:255
  1755.1 127.8 %reduce-scatter.43.cloned.1.call-done = f32[384,48]{0,1:T(8,128)} async-done(((f32[384,768]{0,1:T(8,128)}), f32[384,48]{0,1:T(8,128)}) %reduce-scatter.43.cloned.1.call-update) | async-done | bytes 73744 | tf_op jit(solution)/shard_map/reduce_scatter | solution.py:256
  1882.9 135.1 %reduce-scatter.49.cloned.1.call-done = f32[48,1024]{1,0:T(8,128)} async-done(((f32[768,1024]{1,0:T(8,128)}), f32[48,1024]{1,0:T(8,128)}) %reduce-scatter.49.cloned.1.call-update) | async-done | bytes 196624 | tf_op jit(solution)/shard_map/reduce_scatter | solution.py:261
  2018.0 135.4 %reduce-scatter.51.cloned.1.call-done = f32[48,1024]{1,0:T(8,128)} async-done(((f32[768,1024]{1,0:T(8,128)}), f32[48,1024]{1,0:T(8,128)}) %reduce-scatter.51.cloned.1.call-update) | async-done | bytes 196624 | tf_op jit(solution)/shard_map/reduce_scatter | solution.py:262
  2153.4 135.5 %reduce-scatter.53.cloned.1.call-done = f32[1024,48]{0,1:T(8,128)} async-done(((f32[1024,768]{0,1:T(8,128)}), f32[1024,48]{0,1:T(8,128)}) %reduce-scatter.53.cloned.1.call-update) | async-done | bytes 196624 | tf_op jit(solution)/shard_map/reduce_scatter | solution.py:263
  (323 shorter events, 52.4 us)
Async XLA Ops:
  8.0 56.6 %copy-start = (f32[32,12]{0,1:T(8,128)S(1)}, f32[32,12]{0,1:T(8,128)}, u32[]{:S(2)}) copy-start(f32[32,12]{0,1:T(8,128)} %param.28) | copy-start | bytes 4612
  8.0 591.7 %reduce-scatter.23.cloned.1.call-start = ((), (), s32[]{:S(2)}) async-start(), calls=%async_computation.18 | async-start | bytes 589824 | tf_op jit(solution)/shard_map/reduce_scatter | solution.py:31
  16.1 48.6 %copy-start.95 = (s32[256]{0:T(256)S(1)}, s32[256]{0:T(256)}, u32[]{:S(2)}) copy-start(s32[256]{0:T(256)} %param.43) | copy-start | bytes 3076
  63.8 366.0 %copy-start.67 = (bf16[256,384]{0,1:T(8,128)(2,1)}, bf16[256,384]{0,1:T(8,128)(2,1)S(1)}, u32[]{:S(2)}) copy-start(bf16[256,384]{0,1:T(8,128)(2,1)S(1)} %copy.114) | copy-start | bytes 589828
  282.0 20.6 copy-start.102
  282.0 21.9 copy-start.79
  301.9 42.5 %copy-start.80 = (bf16[48,384]{1,0:T(8,128)(2,1)S(1)}, bf16[48,384]{1,0:T(8,128)(2,1)}, u32[]{:S(2)}) copy-start(bf16[48,384]{1,0:T(8,128)(2,1)} %param.30) | copy-start | bytes 110596
  304.0 122.3 %copy-start.68 = (pred[256,256]{0,1:T(8,128)(4,1)}, pred[256,256]{0,1:T(8,128)(4,1)S(1)}, u32[]{:S(2)}) copy-start(pred[256,256]{0,1:T(8,128)(4,1)S(1)} %fusion.44) | copy-start | bytes 196612
  344.3 43.2 %copy-start.81 = (bf16[384,48]{0,1:T(8,128)(2,1)S(1)}, bf16[384,48]{0,1:T(8,128)(2,1)}, u32[]{:S(2)}) copy-start(bf16[384,48]{0,1:T(8,128)(2,1)} %param.32) | copy-start | bytes 110596
  344.5 85.1 %copy-start.37 = (bf16[256,384]{0,1:T(8,128)(2,1)}, bf16[256,384]{0,1:T(8,128)(2,1)S(1)}, u32[]{:S(2)}) copy-start(bf16[256,384]{0,1:T(8,128)(2,1)S(1)} %copy.115) | copy-start | bytes 589828
  387.5 42.0 %copy-start.39 = (bf16[256,384]{0,1:T(8,128)(2,1)}, bf16[256,384]{0,1:T(8,128)(2,1)S(1)}, u32[]{:S(2)}) copy-start(bf16[256,384]{0,1:T(8,128)(2,1)S(1)} %copy.116) | copy-start | bytes 589828
  426.3 4.6 copy-start.12
  430.8 44.6 %copy-start.63 = (bf16[6,64,256]{2,1,0:T(8,128)(2,1)}, bf16[6,64,256]{2,1,0:T(8,128)(2,1)S(1)}, u32[]{:S(2)}) copy-start(bf16[6,64,256]{2,1,0:T(8,128)(2,1)S(1)} %convolution_convert_fusion.12) | copy-start | bytes 589828
  430.8 44.5 %copy-start.83 = (bf16[48,384]{1,0:T(8,128)(2,1)S(1)}, bf16[48,384]{1,0:T(8,128)(2,1)}, u32[]{:S(2)}) copy-start(bf16[48,384]{1,0:T(8,128)(2,1)} %param.35) | copy-start | bytes 110596
  432.0 182.2 %reduce-scatter.25.cloned.1.call-start = ((), (), s32[]{:S(2)}) async-start(), calls=%async_computation.19 | async-start | bytes 589824 | tf_op jit(solution)/shard_map/reduce_scatter | solution.py:31
  434.0 80.4 %copy-start.23 = (bf16[128,768]{1,0:T(8,128)(2,1)}, bf16[128,768]{1,0:T(8,128)(2,1)S(1)}, u32[]{:S(2)}) copy-start(bf16[128,768]{1,0:T(8,128)(2,1)S(1)} %all_gather.70) | copy-start | bytes 589828
  434.0 81.3 %copy-start.103 = (s32[16]{0:T(128)S(1)}, s32[16]{0:T(128)}, u32[]{:S(2)}) copy-start(s32[16]{0:T(128)} %param.41) | copy-start | bytes 196
  434.0 82.8 %copy-start.84 = (bf16[48,384]{1,0:T(8,128)(2,1)S(1)}, bf16[48,384]{1,0:T(8,128)(2,1)}, u32[]{:S(2)}) copy-start(bf16[48,384]{1,0:T(8,128)(2,1)} %param.33) | copy-start | bytes 110596
  475.3 38.8 %copy-start.14 = (bf16[768,384]{1,0:T(8,128)(2,1)}, bf16[768,384]{1,0:T(8,128)(2,1)S(1)}, u32[]{:S(2)}) copy-start(bf16[768,384]{1,0:T(8,128)(2,1)S(1)} %all_gather.74) | copy-start | bytes 1769476
  475.4 82.8 %copy-start.85 = (bf16[384,48]{0,1:T(8,128)(2,1)S(1)}, bf16[384,48]{0,1:T(8,128)(2,1)}, u32[]{:S(2)}) copy-start(bf16[384,48]{0,1:T(8,128)(2,1)} %param.36) | copy-start | bytes 110596
  514.1 85.7 %copy-start.2 = (bf16[128,768]{1,0:T(8,128)(2,1)S(1)}, bf16[128,768]{1,0:T(8,128)(2,1)}, u32[]{:S(2)}) copy-start(bf16[128,768]{1,0:T(8,128)(2,1)} %param.22) | copy-start | bytes 589828
  515.0 86.4 %copy-start.76 = (f32[768]{0:T(1024)S(1)}, f32[768]{0:T(1024)}, u32[]{:S(2)}) copy-start(f32[768]{0:T(1024)} %param.26) | copy-start | bytes 9220
  515.4 90.5 %copy-start.61 = (bf16[128,384]{0,1:T(8,128)(2,1)}, bf16[128,384]{0,1:T(8,128)(2,1)S(1)}, u32[]{:S(2)}) copy-start(bf16[128,384]{0,1:T(8,128)(2,1)S(1)} %copy.123) | copy-start | bytes 294916
  516.1 90.2 %copy-start.71 = (bf16[128,384]{0,1:T(8,128)(2,1)}, bf16[128,384]{0,1:T(8,128)(2,1)S(1)}, u32[]{:S(2)}) copy-start(bf16[128,384]{0,1:T(8,128)(2,1)S(1)} %copy.121) | copy-start | bytes 294916
  558.1 47.5 %copy-start.15 = (bf16[768,384]{1,0:T(8,128)(2,1)}, bf16[768,384]{1,0:T(8,128)(2,1)S(1)}, u32[]{:S(2)}) copy-start(bf16[768,384]{1,0:T(8,128)(2,1)S(1)} %all_gather.73) | copy-start | bytes 1769476
  601.4 4.4 copy-start.94
  607.2 4.3 copy-start.49
  607.2 7.0 copy-start.5
  607.9 8.5 copy-start.74
  609.0 58.6 %all-gather.4.cloned.1.call-start = ((), (), s32[]{:S(2)}) async-start(), calls=%async_computation.20 | async-start | bytes 1671168 | tf_op jit(solution)/shard_map/all_gather | solution.py:127
  609.6 117.3 %all-gather.6.cloned.1.call-start = ((), (), s32[]{:S(2)}) async-start(), calls=%async_computation.21 | async-start | bytes 1671168 | tf_op jit(solution)/shard_map/all_gather | solution.py:128
  610.2 176.1 %all-gather.8.cloned.1.call-start = ((), (), s32[]{:S(2)}) async-start(), calls=%async_computation.22 | async-start | bytes 1671168 | tf_op jit(solution)/shard_map/all_gather | solution.py:129
  610.8 189.4 %reduce-scatter.29.cloned.1.call-start = ((), (), s32[]{:S(2)}) async-start(), calls=%async_computation.24 | async-start | bytes 589824 | tf_op jit(solution)/shard_map/reduce_scatter | solution.py:31
  786.3 4.3 copy-start.7
  793.7 29.8 %reduce-scatter.31.cloned.1.call-start = ((), (), s32[]{:S(2)}) async-start(), calls=%async_computation.25 | async-start | bytes 589824 | tf_op jit(solution)/shard_map/reduce_scatter | solution.py:31
  800.2 6.8 copy-start.18
  802.8 7.0 copy-start.97
  814.2 20.1 reduce-scatter.27.cloned.1.call-start
  817.9 52.5 %reduce-scatter.35.cloned.1.call-start = ((), (), s32[]{:S(2)}) async-start(), calls=%async_computation.27 | async-start | bytes 294912 | tf_op jit(solution)/shard_map/reduce_scatter | solution.py:31
  818.0 4.4 copy-start.11
  821.7 12.6 copy-start.25
  821.8 12.6 copy-start.75
  821.8 12.6 copy-start.77
  823.4 15.4 copy-start.13
  823.4 466.8 %reduce-scatter.33.cloned.1.call-start = ((), (), s32[]{:S(2)}) async-start(), calls=%async_computation.26 | async-start | bytes 589824 | tf_op jit(solution)/shard_map/reduce_scatter | solution.py:31
  848.3 486.0 %reduce-scatter.45.cloned.1.call-start = ((), (), s32[]{:S(2)}) async-start(), calls=%async_computation.32 | async-start | bytes 1253376 | tf_op jit(solution)/shard_map/reduce_scatter | solution.py:257
  849.8 484.5 %reduce-scatter.55.cloned.1.call-start = ((), (), s32[]{:S(2)}) async-start(), calls=%async_computation.37 | async-start | bytes 1253376
  851.7 482.7 %reduce-scatter.57.cloned.1.call-start = ((), (), s32[]{:S(2)}) async-start(), calls=%async_computation.38 | async-start | bytes 1253376
  853.5 517.9 %reduce-scatter.47.cloned.1.call-start = ((), (), s32[]{:S(2)}) async-start(), calls=%async_computation.33 | async-start | bytes 1253376 | tf_op jit(solution)/shard_map/reduce_scatter | solution.py:260
  855.0 644.2 %reduce-scatter.37.cloned.1.call-start = ((), (), s32[]{:S(2)}) async-start(), calls=%async_computation.28 | async-start | bytes 1253376 | tf_op jit(solution)/shard_map/reduce_scatter | solution.py:253
  856.6 770.7 %reduce-scatter.39.cloned.1.call-start = ((), (), s32[]{:S(2)}) async-start(), calls=%async_computation.29 | async-start | bytes 1253376 | tf_op jit(solution)/shard_map/reduce_scatter | solution.py:254
  858.1 897.0 %reduce-scatter.41.cloned.1.call-start = ((), (), s32[]{:S(2)}) async-start(), calls=%async_computation.30 | async-start | bytes 1253376 | tf_op jit(solution)/shard_map/reduce_scatter | solution.py:255
  859.7 1023.3 %reduce-scatter.43.cloned.1.call-start = ((), (), s32[]{:S(2)}) async-start(), calls=%async_computation.31 | async-start | bytes 1253376 | tf_op jit(solution)/shard_map/reduce_scatter | solution.py:256
  861.2 1156.8 %reduce-scatter.49.cloned.1.call-start = ((), (), s32[]{:S(2)}) async-start(), calls=%async_computation.34 | async-start | bytes 3342336 | tf_op jit(solution)/shard_map/reduce_scatter | solution.py:261
  863.7 1289.7 %reduce-scatter.51.cloned.1.call-start = ((), (), s32[]{:S(2)}) async-start(), calls=%async_computation.35 | async-start | bytes 3342336 | tf_op jit(solution)/shard_map/reduce_scatter | solution.py:262
  866.9 1422.0 %reduce-scatter.53.cloned.1.call-start = ((), (), s32[]{:S(2)}) async-start(), calls=%async_computation.36 | async-start | bytes 3342336 | tf_op jit(solution)/shard_map/reduce_scatter | solution.py:263
  875.7 414.1 %copy-start.96 = (s32[256]{0:T(256)S(1)}, s32[256]{0:T(256)}, u32[]{:S(2)}) copy-start(s32[256]{0:T(256)} %param.43) | copy-start | bytes 3076
  875.7 414.6 %copy-start.78 = (f32[768]{0:T(1024)S(1)}, f32[768]{0:T(1024)}, u32[]{:S(2)}) copy-start(f32[768]{0:T(1024)} %param.25) | copy-start | bytes 9220
  875.7 414.6 %copy-start.92 = (f32[128]{0:T(128)S(1)}, f32[128]{0:T(128)}, u32[]{:S(2)}) copy-start(f32[128]{0:T(128)} %copy-done.91) | copy-start | bytes 1540
  875.7 415.7 %copy-start.88 = (f32[768]{0:T(1024)S(1)}, f32[768]{0:T(1024)}, u32[]{:S(2)}) copy-start(f32[768]{0:T(1024)} %get-tuple-element.90) | copy-start | bytes 9220
  875.7 415.7 %copy-start.89 = (f32[768]{0:T(1024)S(1)}, f32[768]{0:T(1024)}, u32[]{:S(2)}) copy-start(f32[768]{0:T(1024)} %get-tuple-element.92) | copy-start | bytes 9220
  875.7 456.8 %copy-start.99 = (f32[128]{0:T(128)S(1)}, f32[128]{0:T(128)}, u32[]{:S(2)}) copy-start(f32[128]{0:T(128)} %copy-done.98) | copy-start | bytes 1540
  875.7 456.8 %copy-start.54 = (f32[128,768]{1,0:T(8,128)S(1)}, f32[128,768]{1,0:T(8,128)}, u32[]{:S(2)}) copy-start(f32[128,768]{1,0:T(8,128)} %get-tuple-element.101) | copy-start | bytes 1179652
  875.7 1413.2 %copy-start.1 = (f32[32,12]{0,1:T(8,128)S(1)}, f32[32,12]{0,1:T(8,128)}, u32[]{:S(2)}) copy-start(f32[32,12]{0,1:T(8,128)} %param.28) | copy-start | bytes 4612
  (61 other events, 76.7 us)
Sparse Core Ops, SparseCore 0:
  432.1 5.4 reduce-scatter.22
  609.2 4.9 reduce-scatter.24
  793.9 6.3 reduce-scatter.28
  814.3 8.9 reduce-scatter.30
  825.3 8.9 reduce-scatter.26
  836.5 8.7 reduce-scatter.34
  848.4 8.9 reduce-scatter.32
  862.7 124.7 reduce-scatter.44
  992.9 122.6 reduce-scatter.54
  1120.7 122.6 reduce-scatter.56
  1248.8 122.6 reduce-scatter.46
  1376.6 122.6 reduce-scatter.36
  1504.6 122.6 reduce-scatter.38
  1632.5 122.6 reduce-scatter.40
  1760.3 122.6 reduce-scatter.42
  1888.4 129.6 reduce-scatter.48
  2023.4 129.9 reduce-scatter.50
  2158.8 130.0 reduce-scatter.52
Sparse Core Ops, SparseCore 1:
  612.3 55.3 all-gather.3
  670.3 56.6 all-gather.5
  729.6 56.6 all-gather.7
where the time goes:
time: 2300 us
  waiting for transfers between devices  1130 us (49%)
  other arithmetic  425 us (18%)
  blocking collectives  385 us (17%)
  local copies, waits for them, and re-layouts  282 us (12%)
  matrix products  53.9 us (2%)
    scatter-add x1, other arithmetic, build_extra(): return jnp.transpose(per_dist[distance], (2, 0, 1))  396 us
    gather x2, local copies, waits for them, and re-layouts, build_extra(): return jnp.transpose(per_dist[distance], (2, 0, 1))  237 us
    reduce_scatter x1, waiting for transfers between devices, shards(): lax.psum_scatter(grad_down, 'dp', scatter_dimension=1, tiled=True)  135 us
    reduce_scatter x1, waiting for transfers between devices, shards(): lax.psum_scatter(grad_up, 'dp', scatter_dimension=0, tiled=True)  135 us
    reduce_scatter x1, waiting for transfers between devices, shards(): lax.psum_scatter(grad_gate, 'dp', scatter_dimension=0, tiled=True)  135 us
    reduce_scatter x1, waiting for transfers between devices, shards(): lax.psum_scatter(grad_w_key, 'dp', scatter_dimension=0, tiled=True)  128 us
    reduce_scatter x1, waiting for transfers between devices, shards(): lax.psum_scatter(grad_w_query, 'dp', scatter_dimension=0, tiled=True)  128 us
    reduce_scatter x1, waiting for transfers between devices, shards(): lax.psum_scatter(grad_w_value, 'dp', scatter_dimension=0, tiled=True)  128 us
  transfers between devices with their start and end apart: 21, of which 13 were waited for; matrix products, arithmetic and copies ran while one was open for 21% of the time, Pallas kernels for 0%

commit v1 on v0

v1 whole, which is shorter than its diff:
```python
import functools

import jax
import jax.numpy as jnp
from jax import lax
from jax.experimental import pallas as pl
from jax.experimental.pallas import tpu as pltpu
from jax.sharding import PartitionSpec as P

H = 12
DH = 64
NB = 32
LEN = 256
ENC = 128
EPSILON = 1e-06
NEGATIVE = -1e30
F32 = jnp.float32
BF16 = jnp.bfloat16
VMEM_LIMIT = 56 * 1024 * 1024


def product(left, right):
    return jnp.dot(left, right, preferred_element_type=F32)


def product_tn(left, right):
    return lax.dot_general(left, right, (((0,), (0,)), ((), ())), preferred_element_type=F32)


def product_nt(left, right):
    return lax.dot_general(left, right, (((1,), (1,)), ((), ())), preferred_element_type=F32)


def exact_nt(left, right):
    return lax.dot_general(
        left, right, (((1,), (1,)), ((), ())), preferred_element_type=F32, precision=lax.Precision.HIGHEST
    )


def inverse_rms(values):
    return lax.rsqrt(jnp.mean(values * values, axis=-1, keepdims=True) + EPSILON)


def norm_back(values, gain, upstream):
    inverse = inverse_rms(values)
    scaled = upstream * gain
    inner = jnp.mean(scaled * values, axis=-1, keepdims=True)
    grad_values = inverse * scaled - values * (inverse * inverse * inverse * inner)
    grad_gain = jnp.sum(upstream * values * inverse, axis=0, keepdims=True)
    return grad_values, grad_gain


def both_heads(pair):
    first = lax.broadcasted_iota(jnp.int32, pair.shape, 1) < DH
    zero = jnp.zeros_like(pair)
    return jnp.concatenate([jnp.where(first, pair, zero), jnp.where(first, zero, pair)], axis=0)


def join_heads(stacked):
    rows = stacked.shape[0] // 2
    first = lax.broadcasted_iota(jnp.int32, (rows, stacked.shape[1]), 1) < DH
    return jnp.where(first, stacked[:rows], stacked[rows:])


def softmax(scores):
    expo = jnp.exp(scores - jnp.max(scores, axis=-1, keepdims=True))
    return expo * (1.0 / jnp.sum(expo, axis=-1, keepdims=True))


def attend_back(query, keys, values, probs, upstream):
    upper = both_heads(upstream)
    grad_probs = product_nt(upper, values)
    inner = jnp.sum(probs * grad_probs, axis=-1, keepdims=True)
    grad_scores = (probs * (grad_probs - inner)).astype(BF16)
    grad_query = join_heads(product(grad_scores, keys)).astype(BF16)
    grad_keys = product_tn(grad_scores, both_heads(query)).astype(BF16)
    grad_values = product_tn(probs.astype(BF16), upper).astype(BF16)
    return grad_query, grad_keys, grad_values, grad_scores


def bucket_onehot(buckets):
    return (lax.broadcasted_iota(jnp.int32, (NB, LEN), 0) == buckets).astype(F32)


def reversal():
    shape = (LEN, LEN)
    return (
        lax.broadcasted_iota(jnp.int32, shape, 0) + lax.broadcasted_iota(jnp.int32, shape, 1) == LEN - 1
    ).astype(BF16)


class Plan:
    def __init__(self, mesh, rows):
        self.size = mesh.shape["dp"]
        self.rows = rows
        self.staged = self.size == 16 and rows % 16 == 0
        self.pieces = 8 if self.staged else 1

    def place(self):
        index = lax.axis_index("dp")
        return index >> 2, (index >> 1) & 1, index & 1

    def spans(self, forward):
        if not self.staged:
            return [(0, 0, 0, self.size * self.rows, None)]
        z, y, x = self.place()
        sign = -1 if forward else 1
        result = []
        for way in range(4):
            dy, dx = way >> 1, way & 1
            for step in range(4):
                source = ((z + sign * step) & 3) * 4 + (y ^ dy) * 2 + (x ^ dx)
                first = pl.multiple_of(source * self.rows, 16)
                for half in range(2):
                    result.append((2 * way + half, step * self.rows, first, self.rows, half))
        return result

    def copies(self, pieces, whole, sems, forward):
        width = whole.shape[1] // 2
        result = []
        for number, (piece, row, first, rows, half) in enumerate(self.spans(forward)):
            columns = pl.ds(0, 2 * width) if half is None else pl.ds(half * width, width)
            part = pieces[piece].at[pl.ds(row, rows), :]
            block = whole.at[pl.ds(first, rows), columns]
            ends = (part, block) if forward else (block, part)
            result.append(pltpu.make_async_copy(*ends, sems.at[number]))
        return result

    def n_copies(self):
        return 32 if self.staged else 1

    def piece_shapes(self, width):
        if self.staged:
            return [jax.ShapeDtypeStruct((4 * self.rows, width // 2), BF16)] * 8
        return [jax.ShapeDtypeStruct((self.size * self.rows, width), BF16)]


def swap(block, axis_bit, size):
    return lax.ppermute(block, "dp", [(i, i ^ axis_bit) for i in range(size)])


def shift_z(block, step):
    return lax.ppermute(block, "dp", [(i, (((i >> 2) + step) & 3) * 4 + (i & 3)) for i in range(16)])


def gather(plan, block):
    if not plan.staged:
        return [lax.all_gather(block, "dp", axis=0, tiled=True)]
    column = jnp.concatenate([block] + [shift_z(block, step) for step in (1, 2, 3)], axis=0)
    half = block.shape[1] // 2
    one, two = column[:, :half], column[:, half:]
    one_x = swap(one, 1, 16)
    two_y = swap(two, 2, 16)
    one_y = swap(one, 2, 16)
    two_x = swap(two, 1, 16)
    one_d = swap(one_x, 2, 16)
    two_d = swap(two_y, 1, 16)
    return [one, two, one_x, two_x, one_y, two_y, one_d, two_d]


def scatter_sum(plan, pieces):
    if not plan.staged:
        return [lax.psum_scatter(pieces[0].astype(F32), "dp", scatter_dimension=0, tiled=True)]
    one, two, one_x, two_x, one_y, two_y, one_d, two_d = pieces
    wide = lambda value: value.astype(F32)
    got_d1 = swap(one_d, 2, 16)
    got_d2 = swap(two_d, 1, 16)
    got_y1 = swap(one_y, 2, 16)
    got_x2 = swap(two_x, 1, 16)
    got_x1 = swap((wide(one_x) + wide(got_d1)).astype(BF16), 1, 16)
    got_y2 = swap((wide(two_y) + wide(got_d2)).astype(BF16), 2, 16)
    total = jnp.concatenate(
        [
            (wide(one) + wide(got_y1) + wide(got_x1)).astype(BF16),
            (wide(two) + wide(got_x2) + wide(got_y2)).astype(BF16),
        ],
        axis=1,
    )
    rows = plan.rows
    return [total[:rows]] + [shift_z(total[step * rows : (step + 1) * rows], step) for step in (1, 2, 3)]


def other_core(block):
    return lax.ppermute(block, "tensor", [(0, 1), (1, 0)])


def sum_everywhere(plan, block):
    if plan.size & (plan.size - 1):
        return lax.psum(block, ("dp", "tensor"))
    total = block + other_core(block)
    bit = 1
    while bit < plan.size:
        total = total + swap(total, bit, plan.size)
        bit *= 2
    return total


VM = pl.BlockSpec(memory_space=pltpu.VMEM)
SM = pl.BlockSpec(memory_space=pltpu.SMEM)
ANY = pl.BlockSpec(memory_space=pl.ANY)


def call(body, name, inputs, specs, outputs, out_specs, scratch, flops):
    nbytes = sum(a.size * a.dtype.itemsize for a in inputs) + sum(
        a.size * jnp.dtype(a.dtype).itemsize for a in outputs
    )
    return pl.pallas_call(
        body,
        name=name,
        out_shape=outputs,
        in_specs=specs,
        out_specs=out_specs,
        scratch_shapes=scratch,
        compiler_params=pltpu.CompilerParams(vmem_limit_bytes=VMEM_LIMIT),
        cost_estimate=pl.CostEstimate(flops=flops, bytes_accessed=nbytes, transcendentals=0),
    )(*inputs)


def shape(*dims, dtype=F32):
    return jax.ShapeDtypeStruct(dims, dtype)


def rows_of(mine, other, core):
    first = jnp.where(core == 0, mine, other)
    second = jnp.where(core == 0, other, mine)
    return jnp.concatenate([first, second], axis=0)


def wide_sum(mine, other):
    return mine[...].astype(F32) + other[...].astype(F32)


def turned(matrix):
    n = matrix.shape[0]
    eye = (
        lax.broadcasted_iota(jnp.int32, (n, n), 0) == lax.broadcasted_iota(jnp.int32, (n, n), 1)
    ).astype(BF16)
    return product_tn(matrix, eye).astype(BF16)


def pack_attention(plan, query, key, value, out):
    rows, width = query.shape
    if rows % 16:
        return jnp.concatenate([query, key, value, out.T], axis=1)

    def body(q, k, v, o, packed):
        packed[:, :width] = q[...]
        packed[:, width : 2 * width] = k[...]
        packed[:, 2 * width : 3 * width] = v[...]
        packed[:, 3 * width :] = turned(o[...])

    return call(
        body, "pack", [query, key, value, out], [VM] * 4, shape(rows, 4 * width, dtype=BF16), VM, [], 1 << 20
    ) if False else pl.pallas_call(
        body,
        name="pack_attention",
        out_shape=shape(rows, 4 * width, dtype=BF16),
        in_specs=[VM] * 4,
        out_specs=VM,
        compiler_params=pltpu.CompilerParams(vmem_limit_bytes=VMEM_LIMIT),
    )(query, key, value, out)


def pack_feed(plan, gate, up, down):
    rows, width = gate.shape
    half = width // 2
    if rows % 16:
        turned_down = down.T
        return [
            jnp.concatenate([m[:, i * half : (i + 1) * half] for m in (gate, up, turned_down)], axis=1)
            for i in range(2)
        ]

    def body(g, u, d, *packed):
        for i in range(2):
            units = slice(i * half, (i + 1) * half)
            packed[i][:, :half] = g[:, units]
            packed[i][:, half : 2 * half] = u[:, units]
            packed[i][:, 2 * half :] = turned(d[units, :])

    return pl.pallas_call(
        body,
        name="pack_feed",
        out_shape=[shape(rows, 3 * half, dtype=BF16)] * 2,
        in_specs=[VM] * 3,
        out_specs=[VM] * 2,
        compiler_params=pltpu.CompilerParams(vmem_limit_bytes=VMEM_LIMIT),
    )(gate, up, down)


def bring(plan, pieces, whole, sems):
    copies = plan.copies(pieces, whole, sems, True)
    for copy in copies:
        copy.start()
    return copies


def finish(copies):
    for copy in copies:
        copy.wait()


def hand_out(plan, pieces, whole, sems):
    copies = plan.copies(pieces, whole, sems, False)
    for copy in copies:
        copy.start()
    finish(copies)


def self_forward(plan, pieces, x_mine, x_other, gain, table, buckets, dec_lengths, owner):
    n = plan.pieces
    d = x_mine.shape[1]
    width = sum(p.shape[1] for p in pieces[:2]) // 4 if plan.staged else pieces[0].shape[1] // 4
    pairs = width // (2 * DH)

    def body(*refs):
        weights = refs[:n]
        xm, xo, g, tab, buck, lens, own = refs[n : n + 7]
        part, normed_ref, qkv, probs_ref, mixed_ref, whole, sems = refs[n + 7 :]
        copies = bring(plan, weights, whole, sems)
        core = lax.axis_index("tensor")
        length = lens[own[lax.axis_index("dp")]]
        x = rows_of(xm[...], xo[...], core).astype(F32)
        normed = (x * inverse_rms(x) * g[...]).astype(BF16)
        normed_ref[...] = normed
        distances = lax.dot_general(
            tab[...], bucket_onehot(buck[...]), (((1,), (0,)), ((), ())),
            preferred_element_type=F32, precision=lax.Precision.HIGHEST,
        )
        heads = 2 * pairs
        mine = distances[:heads]
        for other in range(1, H // heads):
            mine = jnp.where(core == other, distances[other * heads : (other + 1) * heads], mine)
        row = lax.broadcasted_iota(jnp.int32, (2 * LEN, LEN), 0) & (LEN - 1)
        key = lax.broadcasted_iota(jnp.int32, (2 * LEN, LEN), 1)
        allowed = (key <= row) & (key < length)
        finish(copies)
        qkv[...] = product(normed, whole[:, : 3 * width]).astype(BF16)
        for pair in range(pairs):
            lanes = slice(pair * 128, (pair + 1) * 128)
            query = qkv[:, lanes]
            keys = qkv[:, width + pair * 128 : width + (pair + 1) * 128]
            values = qkv[:, 2 * width + pair * 128 : 2 * width + (pair + 1) * 128]
            extra = jnp.concatenate(
                [
                    pltpu.roll(
                        jnp.broadcast_to(mine[h : h + 1], (LEN, LEN)), 0, 1, stride=1, stride_axis=0
                    )
                    for h in (2 * pair, 2 * pair + 1)
                ],
                axis=0,
            )
            scores = product_nt(both_heads(query), keys) + extra
            probs = softmax(jnp.where(allowed, scores, NEGATIVE))
            probs_ref[pl.ds(pair * 2 * LEN, 2 * LEN), :] = probs
            mixed_ref[:, lanes] = join_heads(product(probs.astype(BF16), values)).astype(BF16)
        part[...] = product_nt(mixed_ref[...], whole[:, 3 * width :]).astype(BF16)

    outputs = [
        shape(LEN, d, dtype=BF16),
        shape(LEN, d, dtype=BF16),
        shape(LEN, 3 * width, dtype=BF16),
        shape(pairs * 2 * LEN, LEN),
        shape(LEN, width, dtype=BF16),
    ]
    return call(
        body,
        "self_forward",
        [*pieces, x_mine, x_other, gain, table, buckets, dec_lengths, owner],
        [ANY] * n + [VM] * 5 + [SM] * 2,
        outputs,
        [VM] * 5,
        [pltpu.VMEM((d, 4 * width), BF16), pltpu.SemaphoreType.DMA((plan.n_copies(),))],
        2 * LEN * d * 4 * width + 8 * LEN * LEN * width,
    )


def cross_forward(plan, pieces, x_mine, x_other, part_mine, part_other, gain, e_mine, e_other, enc_lengths, owner):
    n = plan.pieces
    d = x_mine.shape[1]
    width = sum(p.shape[1] for p in pieces[:2]) // 4 if plan.staged else pieces[0].shape[1] // 4
    pairs = width // (2 * DH)

    def body(*refs):
        weights = refs[:n]
        xm, xo, pm, po, g, em, eo, lens, own = refs[n : n + 9]
        part, after_ref, normed_ref, q_ref, kv, probs_ref, mixed_ref, whole, sems = refs[n + 9 :]
        copies = bring(plan, weights, whole, sems)
        core = lax.axis_index("tensor")
        length = lens[own[lax.axis_index("dp")]]
        after = rows_of(xm[...], xo[...], core).astype(F32) + wide_sum(pm, po)
        after_ref[...] = after
        normed = (after * inverse_rms(after) * g[...]).astype(BF16)
        normed_ref[...] = normed
        allowed = lax.broadcasted_iota(jnp.int32, (2 * LEN, ENC), 1) < length
        finish(copies)
        kv[...] = product(rows_of(em[...], eo[...], core), whole[:, width : 3 * width]).astype(BF16)
        q_ref[...] = product(normed, whole[:, :width]).astype(BF16)
        for pair in range(pairs):
            lanes = slice(pair * 128, (pair + 1) * 128)
            keys = kv[:, lanes]
            values = kv[:, width + pair * 128 : width + (pair + 1) * 128]
            scores = product_nt(both_heads(q_ref[:, lanes]), keys)
            probs = softmax(jnp.where(allowed, scores, NEGATIVE))
            probs_ref[pl.ds(pair * 2 * LEN, 2 * LEN), :] = probs
            mixed_ref[:, lanes] = join_heads(product(probs.astype(BF16), values)).astype(BF16)
        part[...] = product_nt(mixed_ref[...], whole[:, 3 * width :]).astype(BF16)

    outputs = [
        shape(LEN, d, dtype=BF16),
        shape(LEN, d),
        shape(LEN, d, dtype=BF16),
        shape(LEN, width, dtype=BF16),
        shape(ENC, 2 * width, dtype=BF16),
        shape(pairs * 2 * LEN, ENC),
        shape(LEN, width, dtype=BF16),
    ]
    return call(
        body,
        "cross_forward",
        [*pieces, x_mine, x_other, part_mine, part_other, gain, e_mine, e_other, enc_lengths, owner],
        [ANY] * n + [VM] * 7 + [SM] * 2,
        outputs,
        [VM] * 7,
        [pltpu.VMEM((d, 4 * width), BF16), pltpu.SemaphoreType.DMA((plan.n_copies(),))],
        2 * LEN * d * 3 * width + 4 * LEN * ENC * width,
    )


GELU_C = 0.7978845608028654


def feed_units(normed, top, whole, grads, units):
    gate = product(normed, whole[:, :units])
    upper = product(normed, whole[:, units : 2 * units])
    square = gate * gate
    tanh = jnp.tanh(GELU_C * gate * (1.0 + 0.044715 * square))
    half = 0.5 * (1.0 + tanh)
    gelu = gate * half
    slope = half + 0.5 * gate * (1.0 - tanh * tanh) * (GELU_C * (1.0 + 3 * 0.044715 * square))
    hidden = (gelu * upper).astype(BF16)
    grad_hidden = product(top, whole[:, 2 * units :])
    grad_gate = (grad_hidden * upper * slope).astype(BF16)
    grad_up = (grad_hidden * gelu).astype(BF16)
    out = product_nt(hidden, whole[:, 2 * units :])
    back = product_nt(grad_gate, whole[:, :units]) + product_nt(grad_up, whole[:, units : 2 * units])
    grads[:, :units] = product_tn(normed, grad_gate).astype(BF16)
    grads[:, units : 2 * units] = product_tn(normed, grad_up).astype(BF16)
    grads[:, 2 * units :] = product_tn(top, hidden).astype(BF16)
    return out, back


def feed_first(plan, pieces, after_self, part_mine, part_other, gain, c_mine, c_other, dec_lengths, owner):
    n = plan.pieces
    d = after_self.shape[1]
    total = pieces[0].shape[1] * (2 if plan.staged else 1)
    units = total // 3

    def body(*refs):
        weights = refs[:n]
        a_ref, pm, po, g, cm, co, lens, own = refs[n : n + 8]
        after_ref, normed_ref, top_ref, out_ref, back_ref = refs[n + 8 : n + 13]
        grads_out = refs[n + 13 : 2 * n + 13]
        whole, grads, sems = refs[2 * n + 13 :]
        copies = bring(plan, weights, whole, sems)
        core = lax.axis_index("tensor")
        length = lens[own[lax.axis_index("dp")]]
        after = a_ref[...] + wide_sum(pm, po)
        after_ref[...] = after
        normed = (after * inverse_rms(after) * g[...]).astype(BF16)
        normed_ref[...] = normed
        cot = rows_of(cm[...], co[...], core)
        valid = lax.broadcasted_iota(jnp.int32, cot.shape, 0) < length
        top = jnp.where(valid, cot.astype(F32), 0.0).astype(BF16)
        top_ref[...] = top
        finish(copies)
        out_ref[...], back_ref[...] = feed_units(normed, top, whole, grads, units)
        hand_out(plan, grads_out, grads, sems)

    outputs = [
        shape(LEN, d),
        shape(LEN, d, dtype=BF16),
        shape(LEN, d, dtype=BF16),
        shape(LEN, d),
        shape(LEN, d),
        *plan.piece_shapes(total),
    ]
    return call(
        body,
        "feed_first",
        [*pieces, after_self, part_mine, part_other, gain, c_mine, c_other, dec_lengths, owner],
        [ANY] * n + [VM] * 6 + [SM] * 2,
        outputs,
        [VM] * 5 + [ANY] * n,
        [
            pltpu.VMEM((d, total), BF16),
            pltpu.VMEM((d, total), BF16),
            pltpu.SemaphoreType.DMA((plan.n_copies(),)),
        ],
        2 * LEN * d * 9 * units,
    )


def feed_second(plan, pieces, normed, top, out, back):
    n = plan.pieces
    d = normed.shape[1]
    total = pieces[0].shape[1] * (2 if plan.staged else 1)
    units = total // 3

    def body(*refs):
        weights = refs[:n]
        normed_ref, top_ref, out_ref, back_ref = refs[n : n + 4]
        sums = refs[n + 4]
        grads_out = refs[n + 5 : 2 * n + 5]
        whole, grads, sems = refs[2 * n + 5 :]
        copies = bring(plan, weights, whole, sems)
        finish(copies)
        more_out, more_back = feed_units(normed_ref[...], top_ref[...], whole, grads, units)
        sums[:LEN, :] = (back_ref[...] + more_back).astype(BF16)
        sums[LEN:, :] = (out_ref[...] + more_out).astype(BF16)
        hand_out(plan, grads_out, grads, sems)

    return call(
        body,
        "feed_second",
        [*pieces, normed, top, out, back],
        [ANY] * n + [VM] * 4,
        [shape(2 * LEN, d, dtype=BF16), *plan.piece_shapes(total)],
        [VM] + [ANY] * n,
        [
            pltpu.VMEM((d, total), BF16),
            pltpu.VMEM((d, total), BF16),
            pltpu.SemaphoreType.DMA((plan.n_copies(),)),
        ],
        2 * LEN * d * 9 * units,
    )


def cross_backward(
    plan, pieces, after_cross, top, sums_mine, sums_other, gain, normed, query, kv, probs, mixed, e_mine, e_other
):
    n = plan.pieces
    d = normed.shape[1]
    width = query.shape[1]
    pairs = width // (2 * DH)
    half_rows = LEN // 2

    def body(*refs):
        weights = refs[:n]
        after, top_ref, sm, so, g, normed_ref, q_ref, kv_ref, probs_ref, mixed_ref, em, eo = refs[n : n + 12]
        total_ref, sums, layer_out, grad_gain = refs[n + 12 : n + 16]
        grads_out = refs[n + 16 : 2 * n + 16]
        whole, grads, grad_q, grad_kv, sems = refs[2 * n + 16 :]
        copies = bring(plan, weights, whole, sems)
        core = lax.axis_index("tensor")
        back, gain_row = norm_back(after[...], g[...], wide_sum(sm.at[:LEN], so.at[:LEN]))
        grad_gain[...] = gain_row
        total = top_ref[...].astype(F32) + back
        total_ref[...] = total
        upstream = total.astype(BF16)
        first = pl.multiple_of(core * half_rows, half_rows)
        tail = pl.ds(pl.multiple_of(LEN + core * half_rows, half_rows), half_rows)
        layer_out[...] = (
            after[pl.ds(first, half_rows), :] + sm[tail, :].astype(F32) + so[tail, :].astype(F32)
        ).astype(BF16)
        states = rows_of(em[...], eo[...], core)
        finish(copies)
        grad_mixed = product(upstream, whole[:, 3 * width :]).astype(BF16)
        for pair in range(pairs):
            lanes = slice(pair * 128, (pair + 1) * 128)
            lanes_v = slice(width + pair * 128, width + (pair + 1) * 128)
            gq, gk, gv, _ = attend_back(
                q_ref[:, lanes],
                kv_ref[:, lanes],
                kv_ref[:, lanes_v],
                probs_ref[pl.ds(pair * 2 * LEN, 2 * LEN), :],
                grad_mixed[:, lanes],
            )
            grad_q[:, lanes] = gq
            grad_kv[:, lanes] = gk
            grad_kv[:, lanes_v] = gv
        sums[:LEN, :] = product_nt(grad_q[...], whole[:, :width]).astype(BF16)
        sums[LEN:, :] = product_nt(grad_kv[...], whole[:, width : 3 * width]).astype(BF16)
        grads[:, :width] = product_tn(normed_ref[...], grad_q[...]).astype(BF16)
        grads[:, width : 3 * width] = product_tn(states, grad_kv[...]).astype(BF16)
        grads[:, 3 * width :] = product_tn(upstream, mixed_ref[...]).astype(BF16)
        hand_out(plan, grads_out, grads, sems)

    return call(
        body,
        "cross_backward",
        [*pieces, after_cross, top, sums_mine, sums_other, gain, normed, query, kv, probs, mixed, e_mine, e_other],
        [ANY] * n + [VM] * 12,
        [
            shape(LEN, d),
            shape(LEN + ENC, d, dtype=BF16),
            shape(half_rows, d, dtype=BF16),
            shape(1, d),
            *plan.piece_shapes(4 * width),
        ],
        [VM] * 4 + [ANY] * n,
        [
            pltpu.VMEM((d, 4 * width), BF16),
            pltpu.VMEM((d, 4 * width), BF16),
            pltpu.VMEM((LEN, width), BF16),
            pltpu.VMEM((ENC, 2 * width), BF16),
            pltpu.SemaphoreType.DMA((plan.n_copies(),)),
        ],
        2 * LEN * d * 6 * width + 10 * LEN * ENC * width,
    )


def self_backward(
    plan, pieces, total_cross, after_self, sums_mine, sums_other, gain, normed, qkv, probs, mixed, buckets
):
    n = plan.pieces
    d = normed.shape[1]
    width = mixed.shape[1]
    pairs = width // (2 * DH)
    half_enc = ENC // 2

    def body(*refs):
        weights = refs[:n]
        tc, after, sm, so, g, normed_ref, qkv_ref, probs_ref, mixed_ref, buck = refs[n : n + 10]
        total_ref, sums, states_out, grad_gain, table_out = refs[n + 10 : n + 15]
        grads_out = refs[n + 15 : 2 * n + 15]
        whole, grads, grad_qkv, sems = refs[2 * n + 15 :]
        copies = bring(plan, weights, whole, sems)
        core = lax.axis_index("tensor")
        back, gain_row = norm_back(after[...], g[...], wide_sum(sm.at[:LEN], so.at[:LEN]))
        grad_gain[...] = gain_row
        total = tc[...] + back
        total_ref[...] = total
        upstream = total.astype(BF16)
        tail = pl.ds(pl.multiple_of(LEN + core * half_enc, half_enc), half_enc)
        states_out[...] = sm[tail, :].astype(F32) + so[tail, :].astype(F32)
        finish(copies)
        grad_mixed = product(upstream, whole[:, 3 * width :]).astype(BF16)
        backwards = reversal()
        per_distance = []
        for pair in range(pairs):
            lanes = slice(pair * 128, (pair + 1) * 128)
            lanes_k = slice(width + pair * 128, width + (pair + 1) * 128)
            lanes_v = slice(2 * width + pair * 128, 2 * width + (pair + 1) * 128)
            gq, gk, gv, gs = attend_back(
                qkv_ref[:, lanes],
                qkv_ref[:, lanes_k],
                qkv_ref[:, lanes_v],
                probs_ref[pl.ds(pair * 2 * LEN, 2 * LEN), :],
                grad_mixed[:, lanes],
            )
            grad_qkv[:, lanes] = gq
            grad_qkv[:, lanes_k] = gk
            grad_qkv[:, lanes_v] = gv
            turned_scores = product(gs, backwards)
            for h in range(2):
                rolled = pltpu.roll(
                    turned_scores[h * LEN : (h + 1) * LEN], 0, 1, stride=1, stride_axis=0
                )
                per_distance.append(jnp.sum(rolled, axis=0, keepdims=True))
        sums[...] = product_nt(grad_qkv[...], whole[:, : 3 * width]).astype(BF16)
        per_distance += [jnp.zeros_like(per_distance[0])] * (8 - len(per_distance))
        table_out[...] = exact_nt(jnp.concatenate(per_distance, axis=0), bucket_onehot(buck[...]))
        grads[:, : 3 * width] = product_tn(normed_ref[...], grad_qkv[...]).astype(BF16)
        grads[:, 3 * width :] = product_tn(upstream, mixed_ref[...]).astype(BF16)
        hand_out(plan, grads_out, grads, sems)

    return call(
        body,
        "self_backward",
        [*pieces, total_cross, after_self, sums_mine, sums_other, gain, normed, qkv, probs, mixed, buckets],
        [ANY] * n + [VM] * 10,
        [
            shape(LEN, d),
            shape(LEN, d, dtype=BF16),
            shape(half_enc, d),
            shape(1, d),
            shape(8, NB),
            *plan.piece_shapes(4 * width),
        ],
        [VM] * 5 + [ANY] * n,
        [
            pltpu.VMEM((d, 4 * width), BF16),
            pltpu.VMEM((d, 4 * width), BF16),
            pltpu.VMEM((LEN, 3 * width), BF16),
            pltpu.SemaphoreType.DMA((plan.n_copies(),)),
        ],
        2 * LEN * d * 8 * width + 14 * LEN * LEN * width,
    )


def last_norm(total_self, x_mine, x_other, sums_mine, sums_other, gain, gain_cross_row, gain_feed_row, table):
    d = total_self.shape[1]
    half_rows = LEN // 2
    heads = H // 2

    def body(total, xm, xo, sm, so, g, ggc, ggf, tab, grad_in, small):
        core = lax.axis_index("tensor")
        x = rows_of(xm[...], xo[...], core).astype(F32)
        upstream = wide_sum(sm, so)
        back, gain_row = norm_back(x, g[...], upstream)
        whole = total[...] + back
        grad_in[...] = jnp.where(core == 0, whole[:half_rows], whole[half_rows:])
        small[...] = jnp.zeros_like(small)
        once = (core == 0).astype(F32)
        small[0:1, :] = gain_row * once
        small[1:2, :] = ggc[...] * once
        small[2:3, :] = ggf[...] * once
        small[8 : 8 + heads, :NB] = tab[:heads, :] * once
        small[16 : 16 + heads, :NB] = tab[:heads, :] * (1.0 - once)

    return call(
        body,
        "last_norm",
        [total_self, x_mine, x_other, sums_mine, sums_other, gain, gain_cross_row, gain_feed_row, table],
        [VM] * 9,
        [shape(half_rows, d), shape(24, d)],
        [VM] * 2,
        [],
        1 << 24,
    )


def shards(
    mesh,
    layer_in,
    enc_states,
    cotangent,
    gain_self,
    gain_cross,
    gain_feed,
    bias_table,
    self_query,
    self_key,
    self_value,
    self_out,
    cross_query,
    cross_key,
    cross_value,
    cross_out,
    gate_proj,
    up_proj,
    down_proj,
    dec_lengths,
    enc_lengths,
    seq_owner,
    bucket_table,
):
    plan = Plan(mesh, self_query.shape[0])
    d = layer_in.shape[1]
    g_self, g_cross, g_feed = (g.reshape(1, d) for g in (gain_self, gain_cross, gain_feed))
    w_self = gather(plan, pack_attention(plan, self_query, self_key, self_value, self_out))
    w_cross = gather(plan, pack_attention(plan, cross_query, cross_key, cross_value, cross_out))
    w_feed = [gather(plan, block) for block in pack_feed(plan, gate_proj, up_proj, down_proj)]
    x_other = other_core(layer_in)
    e_other = other_core(enc_states)
    c_other = other_core(cotangent)
    buckets = jnp.concatenate([bucket_table[:1], bucket_table[:0:-1]]).reshape(1, LEN)
    buckets_up = jnp.concatenate([bucket_table[1:], bucket_table[:1]]).reshape(1, LEN)

    part, normed_s, qkv, probs_s, mixed_s = self_forward(
        plan, w_self, layer_in, x_other, g_self, bias_table.T, buckets, dec_lengths, seq_owner
    )
    part, after_self, normed_c, cq, ckv, probs_c, mixed_c = cross_forward(
        plan, w_cross, layer_in, x_other, part, other_core(part), g_cross, enc_states, e_other, enc_lengths, seq_owner
    )
    after_cross, normed_f, top, out, back, *grads_f1 = feed_first(
        plan, w_feed[0], after_self, part, other_core(part), g_feed, cotangent, c_other, dec_lengths, seq_owner
    )
    terms_f1 = scatter_sum(plan, grads_f1)
    sums, *grads_f2 = feed_second(plan, w_feed[1], normed_f, top, out, back)
    terms_f2 = scatter_sum(plan, grads_f2)
    total_cross, sums, layer_out, gain_feed_row, *grads_c = cross_backward(
        plan, w_cross, after_cross, top, sums, other_core(sums), g_feed, normed_c, cq, ckv, probs_c, mixed_c,
        enc_states, e_other,
    )
    terms_c = scatter_sum(plan, grads_c)
    total_self, sums, grad_states, gain_cross_row, table, *grads_s = self_backward(
        plan, w_self, total_cross, after_self, sums, other_core(sums), g_cross, normed_s, qkv, probs_s, mixed_s,
        buckets_up,
    )
    terms_s = scatter_sum(plan, grads_s)
    grad_in, small = last_norm(
        total_self, layer_in, x_other, sums, other_core(sums), g_self, gain_cross_row, gain_feed_row, table
    )
    small = sum_everywhere(plan, small)
    heads = H // 2
    table_grad = jnp.concatenate([small[8 : 8 + heads, :NB], small[16 : 16 + heads, :NB]], axis=0).T

    def summed(terms):
        return functools.reduce(lambda a, b: a + b, [t.astype(F32) for t in terms])

    width = self_query.shape[1]
    grad_s, grad_c = summed(terms_s), summed(terms_c)
    grad_f = [summed(terms_f1), summed(terms_f2)]
    units = grad_f[0].shape[1] // 3

    def columns(block, number, size):
        return block[:, number * size : (number + 1) * size]

    def feed(number):
        return jnp.concatenate([columns(g, number, units) for g in grad_f], axis=1)

    return (
        layer_out,
        grad_in,
        grad_states,
        small[0],
        small[1],
        small[2],
        table_grad,
        columns(grad_s, 0, width),
        columns(grad_s, 1, width),
        columns(grad_s, 2, width),
        columns(grad_s, 3, width).T,
        columns(grad_c, 0, width),
        columns(grad_c, 1, width),
        columns(grad_c, 2, width),
        columns(grad_c, 3, width).T,
        feed(0),
        feed(1),
        feed(2).T,
    )


def solution(mesh):
    rows = P(("dp", "tensor"), None)
    into, out = P("dp", "tensor"), P("tensor", "dp")
    weights = (into, into, into, out, into, into, into, out, into, into, out)
    in_specs = (rows, rows, rows, P(), P(), P(), P(), *weights, P(), P(), P(), P())
    out_specs = (rows, rows, rows, P(), P(), P(), P(), *weights)
    return jax.shard_map(
        functools.partial(shards, mesh), mesh=mesh, in_specs=in_specs, out_specs=out_specs, check_vma=False
    )
```

time: 2300 us -> 292 us (0.13)
  waiting for transfers between devices: 1130 us -> 87.6 us
  other arithmetic: 425 us -> 8.18 us
  blocking collectives: 385 us -> 0 us
  local copies, waits for them, and re-layouts: 282 us -> 14 us
  starting transfers between devices: 1.28 us -> 121 us
  Pallas kernels: 0 us -> 58.1 us
  matrix products: 53.9 us -> 0 us
    reduce_scatter x16 -> x0, waiting for transfers between devices: 968 us -> none  [the longest x1 135 us: shards(): lax.psum_scatter(grad_down, 'dp', scatter_dimension=1, tiled=True)]
    scatter-add x1 -> x0, other arithmetic: 396 us -> none  [build_extra(): return jnp.transpose(per_dist[distance], (2, 0, 1))]
    all_gather x15 -> x0, blocking collectives: 344 us -> none  [the longest x1 46.3 us: shards(): lax.all_gather(self_value, 'dp', axis=0, tiled=True)]
    gather x2 -> x0, local copies, waits for them, and re-layouts: 237 us -> none  [build_extra(): return jnp.transpose(per_dist[distance], (2, 0, 1))]
    all_gather x3 -> x0, waiting for transfers between devices: 161 us -> none  [the longest x1 56.3 us: shards(): lax.all_gather(up_proj, 'dp', axis=0, tiled=True)]
    ppermute x0 -> x85, starting transfers between devices: none -> 121 us  [the longest x24 64.8 us: shift_z(): lax.ppermute(block, 'dp', [(i, ((i >> 2) + step & 3) * 4 + (i & 3)) for i...]
    ppermute x0 -> x85, waiting for transfers between devices: none -> 87.6 us  [the longest x52 72.7 us: swap(): return lax.ppermute(block, 'dp', [(i, i ^ axis_bit) for i in range(size)])]
    pallas_call x0 -> x10, Pallas kernels: none -> 58.1 us  [the longest x7 52.4 us: call(): pl.pallas_call(body, name=name, out_shape=outputs, in_specs=specs, out_sp...]
  transfers between devices with their start and end apart: 21 -> 85, of which waited for: 13 -> 27; matrix products, arithmetic and copies ran while one was open for 21% -> 6% of each run, Pallas kernels for 0% -> 16%
where the time goes in v1:
time: 292 us; the launch traced here: 291 us
  starting transfers between devices  121 us (41%)
  waiting for transfers between devices  87.6 us (30%)
  Pallas kernels  58.1 us (20%)
  local copies, waits for them, and re-layouts  14 us (5%)
  other arithmetic  8.18 us (3%)
    ppermute x52, waiting for transfers between devices, swap(): return lax.ppermute(block, 'dp', [(i, i ^ axis_bit) for i in range(size)])  72.7 us
    ppermute x24, starting transfers between devices, shift_z(): lax.ppermute(block, 'dp', [(i, ((i >> 2) + step & 3) * 4 + (i & 3)) for i...  64.8 us
    ppermute x52, starting transfers between devices, swap(): return lax.ppermute(block, 'dp', [(i, i ^ axis_bit) for i in range(size)])  56.4 us
    pallas_call x7, Pallas kernels, call(): pl.pallas_call(body, name=name, out_shape=outputs, in_specs=specs, out_sp...  52.4 us
    ppermute x24, waiting for transfers between devices, shift_z(): lax.ppermute(block, 'dp', [(i, ((i >> 2) + step & 3) * 4 + (i & 3)) for i...  12.1 us
    unnamed x162, local copies, waits for them, and re-layouts  9.35 us
  transfers between devices with their start and end apart: 85, of which 27 were waited for; matrix products, arithmetic and copies ran while one was open for 6% of the time, Pallas kernels for 16%

profile of v1, /device:TPU:0, one launch (start us, length us, event | category | flops | bytes accessed | tf_op | source)
XLA Modules:
  0.0 290.9 jit_solution(419284571950661220)
XLA Ops:
  0.7 1.5 copy.42.o
  2.2 1.8 pack_attention.3
  4.0 3.0 %collective-permute-start.19 = (bf16[48,1536]{1,0:T(8,128)(2,1)}, bf16[48,1536]{1,0:T(8,128)(2,1)S(1)}, u32[]{:S(2)}, u32[]{:S(2)}) collective-permute-start(bf16[48,1536]{1,0:T(8,128)(2,1)} %pack_attention.3), channel_id=1, source_target_pairs={{0,8},{2,10},{4,12},{6,14},{8,16},{10,18},{12,20},{14,22},{16,24},... | collective-permute-start | bytes 442376 | tf_op jit(solution)/shard_map/ppermute | solution.py:143
  7.1 2.6 collective-permute-start.20
  11.0 1.5 copy.40.o
  12.5 1.8 pack_attention.2
  15.4 1.7 copy.41.d
  17.1 2.0 pack_feed.1
  23.3 2.9 collective-permute-start.2
  26.8 2.3 collective-permute-start.10
  29.3 2.9 %collective-permute-start.11 = (bf16[48,1536]{1,0:T(8,128)(2,1)S(1)}, bf16[48,1536]{1,0:T(8,128)(2,1)S(1)}, u32[]{:S(2)}, u32[]{:S(2)}) collective-permute-start(bf16[48,1536]{1,0:T(8,128)(2,1)S(1)} %copy-done.50), channel_id=1, source_target_pairs={{0,24},{2,26},{4,28},{6,30},{8,0},{10,2},{12,4},{14,6},{16,8},{18,... | collective-permute-start | bytes 442376 | tf_op jit(solution)/shard_map/ppermute | solution.py:143
  32.2 6.4 %collective-permute-done.1 = bf16[48,1536]{1,0:T(8,128)(2,1)S(1)} collective-permute-done((bf16[48,1536]{1,0:T(8,128)(2,1)}, bf16[48,1536]{1,0:T(8,128)(2,1)S(1)}, u32[]{:S(2)}, u32[]{:S(2)}) %collective-permute-start.1) | collective-permute-done | bytes 147488 | tf_op jit(solution)/shard_map/ppermute | solution.py:143
  40.2 1.5 collective-permute-start.25
  41.8 3.1 %collective-permute-start.32 = (bf16[48,1536]{1,0:T(8,128)(2,1)S(1)}, bf16[48,1536]{1,0:T(8,128)(2,1)S(1)}, u32[]{:S(2)}, u32[]{:S(2)}) collective-permute-start(bf16[48,1536]{1,0:T(8,128)(2,1)S(1)} %copy-done.49), channel_id=1, source_target_pairs={{0,8},{2,10},{4,12},{6,14},{8,16},{10,18},{12,20},{14,22},{16,24},... | collective-permute-start | bytes 442376 | tf_op jit(solution)/shard_map/ppermute | solution.py:143
  45.0 3.1 %collective-permute-start.23 = (bf16[192,768]{1,0:T(8,128)(2,1)S(1)}, bf16[192,768]{1,0:T(8,128)(2,1)S(1)}, u32[]{:S(2)}, u32[]{:S(2)}) collective-permute-start(bf16[192,768]{1,0:T(8,128)(2,1)S(1)} %get-tuple-element.161.refs_1_), channel_id=1, source_target_pairs={{0,2},{2,0},{4,6},{6,4},{8,10},{10,8},{12,14},{14,12},{16,18},{18,... | collective-permute-start | bytes 884744 | tf_op jit(solution)/shard_map/ppermute | solution.py:139
  48.0 1.5 collective-permute-start.24
  52.3 3.5 %collective-permute-start.33 = (bf16[48,1536]{1,0:T(8,128)(2,1)S(1)}, bf16[48,1536]{1,0:T(8,128)(2,1)S(1)}, u32[]{:S(2)}, u32[]{:S(2)}) collective-permute-start(bf16[48,1536]{1,0:T(8,128)(2,1)S(1)} %copy-done.49), channel_id=1, source_target_pairs={{0,16},{2,18},{4,20},{6,22},{8,24},{10,26},{12,28},{14,30},{16,0},... | collective-permute-start | bytes 442376 | tf_op jit(solution)/shard_map/ppermute | solution.py:143
  56.0 4.7 %collective-permute-start.34 = (bf16[48,1536]{1,0:T(8,128)(2,1)S(1)}, bf16[48,1536]{1,0:T(8,128)(2,1)S(1)}, u32[]{:S(2)}, u32[]{:S(2)}) collective-permute-start(bf16[48,1536]{1,0:T(8,128)(2,1)S(1)} %copy-done.49), channel_id=1, source_target_pairs={{0,24},{2,26},{4,28},{6,30},{8,0},{10,2},{12,4},{14,6},{16,8},{18,... | collective-permute-start | bytes 442376 | tf_op jit(solution)/shard_map/ppermute | solution.py:143
  60.7 2.0 collective-permute-done.26.refs_6_
  63.1 1.7 collective-permute-start.6
  64.9 6.3 %self_forward.1 = (bf16[256,768]{1,0:T(8,128)(2,1)}, bf16[256,768]{1,0:T(8,128)(2,1)}, bf16[256,1152]{1,0:T(8,128)(2,1)}, f32[1536,256]{1,0:T(8,128)}, bf16[256,384]{1,0:T(8,128)(2,1)}) custom-call(bf16[192,768]{1,0:T(8,128)(2,1)} %copy-done.9, bf16[192,768]{1,0:T(8,128)(2,1)} %copy-done.8, bf16[192,768]{1,0:T(8,128)(2,1)} %copy-done.23, ...), custom_call_target="tpu_custom_call" | custom-call | flops 805306368 | bytes 5904000 | tf_op jit(solution)/shard_map/self_forward/pallas_call | solution.py:207
  71.3 1.7 collective-permute-start.4
  75.5 5.8 %collective-permute-done.4.refs_3_ = bf16[192,768]{1,0:T(8,128)(2,1)S(1)} collective-permute-done((bf16[192,768]{1,0:T(8,128)(2,1)S(1)}, bf16[192,768]{1,0:T(8,128)(2,1)S(1)}, u32[]{:S(2)}, u32[]{:S(2)}) %collective-permute-start.4) | collective-permute-done | bytes 294944 | tf_op jit(solution)/shard_map/ppermute | solution.py:139
  81.3 1.7 collective-permute-done.5.refs_4_
  83.6 4.3 %collective-permute-done.7.refs_6_ = bf16[192,768]{1,0:T(8,128)(2,1)S(1)} collective-permute-done((bf16[192,768]{1,0:T(8,128)(2,1)S(1)}, bf16[192,768]{1,0:T(8,128)(2,1)S(1)}, u32[]{:S(2)}, u32[]{:S(2)}) %collective-permute-start.7) | collective-permute-done | bytes 294944 | tf_op jit(solution)/shard_map/ppermute | solution.py:139
  88.2 1.6 collective-permute-start.12
  91.1 5.7 %cross_forward.1 = (bf16[256,768]{1,0:T(8,128)(2,1)}, f32[256,768]{1,0:T(8,128)}, bf16[256,768]{1,0:T(8,128)(2,1)}, bf16[256,384]{1,0:T(8,128)(2,1)}, bf16[128,7...) custom-call(bf16[192,768]{1,0:T(8,128)(2,1)} %copy-done.1, bf16[192,768]{1,0:T(8,128)(2,1)} %copy-done, ...), custom_call_target="tpu_custom_call" | custom-call | flops 503316480 | bytes 6687872 | tf_op jit(solution)/shard_map/cross_forward/pallas_call | solution.py:207
  98.4 1.7 collective-permute-start.35
  102.5 5.9 %collective-permute-done.35.refs_2_ = bf16[192,768]{1,0:T(8,128)(2,1)S(1)} collective-permute-done((bf16[192,768]{1,0:T(8,128)(2,1)S(1)}, bf16[192,768]{1,0:T(8,128)(2,1)S(1)}, u32[]{:S(2)}, u32[]{:S(2)}) %collective-permute-start.35) | collective-permute-done | bytes 294944 | tf_op jit(solution)/shard_map/ppermute | solution.py:139
  108.3 1.7 collective-permute-start.36
  111.2 5.1 %collective-permute-done.16.refs_6_ = bf16[192,768]{1,0:T(8,128)(2,1)S(1)} collective-permute-done((bf16[192,768]{1,0:T(8,128)(2,1)S(1)}, bf16[192,768]{1,0:T(8,128)(2,1)S(1)}, u32[]{:S(2)}, u32[]{:S(2)}) %collective-permute-start.16) | collective-permute-done | bytes 294944 | tf_op jit(solution)/shard_map/ppermute | solution.py:139
  119.2 9.0 %feed_first.1 = (f32[256,768]{1,0:T(8,128)}, bf16[256,768]{1,0:T(8,128)(2,1)}, bf16[256,768]{1,0:T(8,128)(2,1)}, f32[256,768]{1,0:T(8,128)}, f32[256,768]{1,0:T(...) custom-call(bf16[192,768]{1,0:T(8,128)(2,1)} %copy-done.43, ...), custom_call_target="tpu_custom_call" | custom-call | flops 1811939328 | bytes 9833600 | tf_op jit(solution)/shard_map/feed_first/pallas_call | solution.py:207
  128.2 1.8 collective-permute-start.71
  134.4 8.2 %feed_second.1 = (bf16[512,768]{1,0:T(8,128)(2,1)}, bf16[192,768]{1,0:T(8,128)(2,1)}, bf16[192,768]{1,0:T(8,128)(2,1)}, bf16[192,768]{1,0:T(8,128)(2,1)}, bf16[1...) custom-call(bf16[192,768]{1,0:T(8,128)(2,1)} %copy-done.46, ...), custom_call_target="tpu_custom_call" | custom-call | flops 1811939328 | bytes 7864320 | tf_op jit(solution)/shard_map/feed_second/pallas_call | solution.py:207
  142.6 1.8 collective-permute-start.80
  146.0 5.9 %collective-permute-done.80 = bf16[192,768]{1,0:T(8,128)(2,1)S(1)} collective-permute-done((bf16[192,768]{1,0:T(8,128)(2,1)}, bf16[192,768]{1,0:T(8,128)(2,1)S(1)}, u32[]{:S(2)}, u32[]{:S(2)}) %collective-permute-start.80) | collective-permute-done | bytes 294944 | tf_op jit(solution)/shard_map/ppermute | solution.py:139
  152.5 2.5 collective-permute-done.77
  159.4 2.4 collective-permute-done.69
  163.0 4.8 %collective-permute-start.73 = (bf16[48,1536]{1,0:T(8,128)(2,1)S(1)}, bf16[48,1536]{1,0:T(8,128)(2,1)S(1)}, u32[]{:S(2)}, u32[]{:S(2)}) collective-permute-start(bf16[48,1536]{1,0:T(8,128)(2,1)S(1)} %get-tuple-element.147), channel_id=1, source_target_pairs={{0,8},{2,10},{4,12},{6,14},{8,16},{10,18},{12,20},{14,22},{16,24},... | collective-permute-start | bytes 442376 | tf_op jit(solution)/shard_map/ppermute | solution.py:143
  167.8 1.5 collective-permute-done.81
  169.3 3.7 %collective-permute-start.74 = (bf16[48,1536]{1,0:T(8,128)(2,1)S(1)}, bf16[48,1536]{1,0:T(8,128)(2,1)S(1)}, u32[]{:S(2)}, u32[]{:S(2)}) collective-permute-start(bf16[48,1536]{1,0:T(8,128)(2,1)S(1)} %get-tuple-element.149), channel_id=1, source_target_pairs={{0,16},{2,18},{4,20},{6,22},{8,24},{10,26},{12,28},{14,30},{16,0},... | collective-permute-start | bytes 442376 | tf_op jit(solution)/shard_map/ppermute | solution.py:143
  173.1 3.4 %collective-permute-start.75 = (bf16[48,1536]{1,0:T(8,128)(2,1)S(1)}, bf16[48,1536]{1,0:T(8,128)(2,1)S(1)}, u32[]{:S(2)}, u32[]{:S(2)}) collective-permute-start(bf16[48,1536]{1,0:T(8,128)(2,1)S(1)} %get-tuple-element.148), channel_id=1, source_target_pairs={{0,24},{2,26},{4,28},{6,30},{8,0},{10,2},{12,4},{14,6},{16,8},{18,... | collective-permute-start | bytes 442376 | tf_op jit(solution)/shard_map/ppermute | solution.py:143
  177.4 2.0 collective-permute-done.74
  179.3 10.1 %collective-permute-start.84 = (bf16[48,1536]{1,0:T(8,128)(2,1)S(1)}, bf16[48,1536]{1,0:T(8,128)(2,1)S(1)}, u32[]{:S(2)}, u32[]{:S(2)}) collective-permute-start(bf16[48,1536]{1,0:T(8,128)(2,1)S(1)} %get-tuple-element.151), channel_id=1, source_target_pairs={{0,24},{2,26},{4,28},{6,30},{8,0},{10,2},{12,4},{14,6},{16,8},{18,... | collective-permute-start | bytes 442376 | tf_op jit(solution)/shard_map/ppermute | solution.py:143
  189.6 3.3 %collective-permute-done.83 = bf16[48,1536]{1,0:T(8,128)(2,1)S(1)} collective-permute-done((bf16[48,1536]{1,0:T(8,128)(2,1)S(1)}, bf16[48,1536]{1,0:T(8,128)(2,1)S(1)}, u32[]{:S(2)}, u32[]{:S(2)}) %collective-permute-start.83) | collective-permute-done | bytes 147488 | tf_op jit(solution)/shard_map/ppermute | solution.py:143
  193.9 9.9 %cross_backward.1 = (f32[256,768]{1,0:T(8,128)}, bf16[384,768]{1,0:T(8,128)(2,1)}, bf16[128,768]{1,0:T(8,128)(2,1)}, f32[1,768]{1,0:T(1,128)}, bf16[192,768]{1,0...) custom-call(bf16[192,768]{1,0:T(8,128)(2,1)} %copy-done.1, ...), custom_call_target="tpu_custom_call" | custom-call | flops 1031798784 | bytes 11016192 | tf_op jit(solution)/shard_map/cross_backward/pallas_call | solution.py:207
  203.8 1.5 collective-permute-start.62
  208.2 5.8 %collective-permute-done.62 = bf16[192,768]{1,0:T(8,128)(2,1)S(1)} collective-permute-done((bf16[192,768]{1,0:T(8,128)(2,1)}, bf16[192,768]{1,0:T(8,128)(2,1)S(1)}, u32[]{:S(2)}, u32[]{:S(2)}) %collective-permute-start.62) | collective-permute-done | bytes 294944 | tf_op jit(solution)/shard_map/ppermute | solution.py:139
  218.5 1.8 collective-permute-done.61
  220.3 3.6 %collective-permute-done.63 = bf16[192,768]{1,0:T(8,128)(2,1)S(1)} collective-permute-done((bf16[192,768]{1,0:T(8,128)(2,1)S(1)}, bf16[192,768]{1,0:T(8,128)(2,1)S(1)}, u32[]{:S(2)}, u32[]{:S(2)}) %collective-permute-start.63) | collective-permute-done | bytes 294944 | tf_op jit(solution)/shard_map/ppermute | solution.py:139
  224.9 10.5 %self_backward.1 = (f32[256,768]{1,0:T(8,128)}, bf16[256,768]{1,0:T(8,128)(2,1)}, f32[64,768]{1,0:T(8,128)}, f32[1,768]{1,0:T(1,128)}, f32[8,32]{1,0:T(8,128)}, ...) custom-call(bf16[192,768]{1,0:T(8,128)(2,1)} %copy-done.9, ...), custom_call_target="tpu_custom_call" | custom-call | flops 1560281088 | bytes 11608064 | tf_op jit(solution)/shard_map/self_backward/pallas_call | solution.py:207
  235.4 1.6 collective-permute-start.53
  238.1 3.1 %collective-permute-start.64 = (bf16[48,1536]{1,0:T(8,128)(2,1)S(1)}, bf16[48,1536]{1,0:T(8,128)(2,1)S(1)}, u32[]{:S(2)}, u32[]{:S(2)}) collective-permute-start(bf16[48,1536]{1,0:T(8,128)(2,1)S(1)} %get-tuple-element.153), channel_id=1, source_target_pairs={{0,8},{2,10},{4,12},{6,14},{8,16},{10,18},{12,20},{14,22},{16,24},... | collective-permute-start | bytes 442376 | tf_op jit(solution)/shard_map/ppermute | solution.py:143
  241.3 3.4 %collective-permute-start.65 = (bf16[48,1536]{1,0:T(8,128)(2,1)S(1)}, bf16[48,1536]{1,0:T(8,128)(2,1)S(1)}, u32[]{:S(2)}, u32[]{:S(2)}) collective-permute-start(bf16[48,1536]{1,0:T(8,128)(2,1)S(1)} %get-tuple-element.155), channel_id=1, source_target_pairs={{0,16},{2,18},{4,20},{6,22},{8,24},{10,26},{12,28},{14,30},{16,0},... | collective-permute-start | bytes 442376 | tf_op jit(solution)/shard_map/ppermute | solution.py:143
  244.7 3.7 %collective-permute-start.66 = (bf16[48,1536]{1,0:T(8,128)(2,1)S(1)}, bf16[48,1536]{1,0:T(8,128)(2,1)S(1)}, u32[]{:S(2)}, u32[]{:S(2)}) collective-permute-start(bf16[48,1536]{1,0:T(8,128)(2,1)S(1)} %get-tuple-element.154), channel_id=1, source_target_pairs={{0,24},{2,26},{4,28},{6,30},{8,0},{10,2},{12,4},{14,6},{16,8},{18,... | collective-permute-start | bytes 442376 | tf_op jit(solution)/shard_map/ppermute | solution.py:143
  248.5 1.9 collective-permute-start.52
  250.4 2.8 last_norm.1
  256.1 1.5 collective-permute-start.54
  259.7 8.0 %collective-permute-done.45 = f32[24,768]{1,0:T(8,128)S(1)} collective-permute-done((f32[24,768]{1,0:T(8,128)S(1)}, f32[24,768]{1,0:T(8,128)S(1)}, u32[]{:S(2)}, u32[]{:S(2)}) %collective-permute-start.45) | collective-permute-done | bytes 73760 | tf_op jit(solution)/shard_map/ppermute | solution.py:139
  268.4 2.4 collective-permute-done.54
  271.5 3.5 %collective-permute-start.57 = (bf16[48,1536]{1,0:T(8,128)(2,1)S(1)}, bf16[48,1536]{1,0:T(8,128)(2,1)S(1)}, u32[]{:S(2)}, u32[]{:S(2)}) collective-permute-start(bf16[48,1536]{1,0:T(8,128)(2,1)S(1)} %get-tuple-element.157), channel_id=1, source_target_pairs={{0,24},{2,26},{4,28},{6,30},{8,0},{10,2},{12,4},{14,6},{16,8},{18,... | collective-permute-start | bytes 442376 | tf_op jit(solution)/shard_map/ppermute | solution.py:143
  276.4 8.0 %collective-permute-done.47 = f32[24,768]{1,0:T(8,128)S(1)} collective-permute-done((f32[24,768]{1,0:T(8,128)S(1)}, f32[24,768]{1,0:T(8,128)S(1)}, u32[]{:S(2)}, u32[]{:S(2)}) %collective-permute-start.47) | collective-permute-done | bytes 73760 | tf_op jit(solution)/shard_map/ppermute | solution.py:139
  284.4 1.5 collective-permute-start.48
  286.7 3.0 %collective-permute-done.48 = f32[24,768]{1,0:T(8,128)S(1)} collective-permute-done((f32[24,768]{1,0:T(8,128)S(1)}, f32[24,768]{1,0:T(8,128)S(1)}, u32[]{:S(2)}, u32[]{:S(2)}) %collective-permute-start.48) | collective-permute-done | bytes 73760 | tf_op jit(solution)/shard_map/ppermute | solution.py:139
  (332 shorter events, 58.0 us)
Async XLA Ops:
  4.0 19.3 %collective-permute-start.19 = (bf16[48,1536]{1,0:T(8,128)(2,1)}, bf16[48,1536]{1,0:T(8,128)(2,1)S(1)}, u32[]{:S(2)}, u32[]{:S(2)}) collective-permute-start(bf16[48,1536]{1,0:T(8,128)(2,1)} %pack_attention.3), channel_id=1, source_target_pairs={{0,8},{2,10},{4,12},{6,14},{8,16},{10,18},{12,20},{14,22},{16,24},... | collective-permute-start | bytes 442376 | tf_op jit(solution)/shard_map/ppermute | solution.py:143
  7.1 19.1 %collective-permute-start.20 = (bf16[48,1536]{1,0:T(8,128)(2,1)}, bf16[48,1536]{1,0:T(8,128)(2,1)S(1)}, u32[]{:S(2)}, u32[]{:S(2)}) collective-permute-start(bf16[48,1536]{1,0:T(8,128)(2,1)} %pack_attention.3), channel_id=1, source_target_pairs={{0,16},{2,18},{4,20},{6,22},{8,24},{10,26},{12,28},{14,30},{16,0},... | collective-permute-start | bytes 442376 | tf_op jit(solution)/shard_map/ppermute | solution.py:143
  9.7 17.2 %collective-permute-start.21 = (bf16[48,1536]{1,0:T(8,128)(2,1)}, bf16[48,1536]{1,0:T(8,128)(2,1)S(1)}, u32[]{:S(2)}, u32[]{:S(2)}) collective-permute-start(bf16[48,1536]{1,0:T(8,128)(2,1)} %pack_attention.3), channel_id=1, source_target_pairs={{0,24},{2,26},{4,28},{6,30},{8,0},{10,2},{12,4},{14,6},{16,8},{18,... | collective-permute-start | bytes 442376 | tf_op jit(solution)/shard_map/ppermute | solution.py:143
  14.4 14.9 %collective-permute-start = (bf16[48,1536]{1,0:T(8,128)(2,1)}, bf16[48,1536]{1,0:T(8,128)(2,1)S(1)}, u32[]{:S(2)}, u32[]{:S(2)}) collective-permute-start(bf16[48,1536]{1,0:T(8,128)(2,1)} %pack_attention.2), channel_id=1, source_target_pairs={{0,8},{2,10},{4,12},{6,14},{8,16},{10,18},{12,20},{14,22},{16,24},... | collective-permute-start | bytes 442376 | tf_op jit(solution)/shard_map/ppermute | solution.py:143
  15.0 23.6 %collective-permute-start.1 = (bf16[48,1536]{1,0:T(8,128)(2,1)}, bf16[48,1536]{1,0:T(8,128)(2,1)S(1)}, u32[]{:S(2)}, u32[]{:S(2)}) collective-permute-start(bf16[48,1536]{1,0:T(8,128)(2,1)} %pack_attention.2), channel_id=1, source_target_pairs={{0,16},{2,18},{4,20},{6,22},{8,24},{10,26},{12,28},{14,30},{16,0},... | collective-permute-start | bytes 442376 | tf_op jit(solution)/shard_map/ppermute | solution.py:143
  23.3 16.8 %collective-permute-start.2 = (bf16[48,1536]{1,0:T(8,128)(2,1)S(1)}, bf16[48,1536]{1,0:T(8,128)(2,1)S(1)}, u32[]{:S(2)}, u32[]{:S(2)}) collective-permute-start(bf16[48,1536]{1,0:T(8,128)(2,1)S(1)} %copy-done.16), channel_id=1, source_target_pairs={{0,24},{2,26},{4,28},{6,30},{8,0},{10,2},{12,4},{14,6},{16,8},{18,... | collective-permute-start | bytes 442376 | tf_op jit(solution)/shard_map/ppermute | solution.py:143
  26.2 15.6 %collective-permute-start.9 = (bf16[48,1536]{1,0:T(8,128)(2,1)}, bf16[48,1536]{1,0:T(8,128)(2,1)S(1)}, u32[]{:S(2)}, u32[]{:S(2)}) collective-permute-start(bf16[48,1536]{1,0:T(8,128)(2,1)} %get-tuple-element.81), channel_id=1, source_target_pairs={{0,8},{2,10},{4,12},{6,14},{8,16},{10,18},{12,20},{14,22},{16,24},... | collective-permute-start | bytes 442376 | tf_op jit(solution)/shard_map/ppermute | solution.py:143
  26.8 18.1 %collective-permute-start.10 = (bf16[48,1536]{1,0:T(8,128)(2,1)}, bf16[48,1536]{1,0:T(8,128)(2,1)S(1)}, u32[]{:S(2)}, u32[]{:S(2)}) collective-permute-start(bf16[48,1536]{1,0:T(8,128)(2,1)} %get-tuple-element.81), channel_id=1, source_target_pairs={{0,16},{2,18},{4,20},{6,22},{8,24},{10,26},{12,28},{14,30},{16,0},... | collective-permute-start | bytes 442376 | tf_op jit(solution)/shard_map/ppermute | solution.py:143
  29.3 18.7 %collective-permute-start.11 = (bf16[48,1536]{1,0:T(8,128)(2,1)S(1)}, bf16[48,1536]{1,0:T(8,128)(2,1)S(1)}, u32[]{:S(2)}, u32[]{:S(2)}) collective-permute-start(bf16[48,1536]{1,0:T(8,128)(2,1)S(1)} %copy-done.50), channel_id=1, source_target_pairs={{0,24},{2,26},{4,28},{6,30},{8,0},{10,2},{12,4},{14,6},{16,8},{18,... | collective-permute-start | bytes 442376 | tf_op jit(solution)/shard_map/ppermute | solution.py:143
  38.7 10.9 %collective-permute-start.22 = (bf16[192,768]{1,0:T(8,128)(2,1)S(1)}, bf16[192,768]{1,0:T(8,128)(2,1)S(1)}, u32[]{:S(2)}, u32[]{:S(2)}) collective-permute-start(bf16[192,768]{1,0:T(8,128)(2,1)S(1)} %get-tuple-element.162.refs_0_), channel_id=1, source_target_pairs={{0,2},{2,0},{4,6},{6,4},{8,10},{10,8},{12,14},{14,12},{16,18},{18,... | collective-permute-start | bytes 884744 | tf_op jit(solution)/shard_map/ppermute | solution.py:139
  45.0 11.0 %collective-permute-start.23 = (bf16[192,768]{1,0:T(8,128)(2,1)S(1)}, bf16[192,768]{1,0:T(8,128)(2,1)S(1)}, u32[]{:S(2)}, u32[]{:S(2)}) collective-permute-start(bf16[192,768]{1,0:T(8,128)(2,1)S(1)} %get-tuple-element.161.refs_1_), channel_id=1, source_target_pairs={{0,2},{2,0},{4,6},{6,4},{8,10},{10,8},{12,14},{14,12},{16,18},{18,... | collective-permute-start | bytes 884744 | tf_op jit(solution)/shard_map/ppermute | solution.py:139
  48.0 12.6 %collective-permute-start.24 = (bf16[192,768]{1,0:T(8,128)(2,1)S(1)}, bf16[192,768]{1,0:T(8,128)(2,1)S(1)}, u32[]{:S(2)}, u32[]{:S(2)}) collective-permute-start(bf16[192,768]{1,0:T(8,128)(2,1)S(1)} %get-tuple-element.162.refs_0_), channel_id=1, source_target_pairs={{0,4},{2,6},{4,0},{6,2},{8,12},{10,14},{12,8},{14,10},{16,20},{18,... | collective-permute-start | bytes 884744 | tf_op jit(solution)/shard_map/ppermute | solution.py:139
  49.6 13.1 %collective-permute-start.26 = (bf16[192,768]{1,0:T(8,128)(2,1)S(1)}, bf16[192,768]{1,0:T(8,128)(2,1)S(1)}, u32[]{:S(2)}, u32[]{:S(2)}) collective-permute-start(bf16[192,768]{1,0:T(8,128)(2,1)S(1)} %collective-permute-done.22.refs_2_), channel_id=1, source_target_pairs={{0,4},{2,6},{4,0},{6,2},{8,12},{10,14},{12,8},{14,10},{16,20},{18,... | collective-permute-start | bytes 884744 | tf_op jit(solution)/shard_map/ppermute | solution.py:139
  50.1 13.0 %collective-permute-start.27 = (bf16[192,768]{1,0:T(8,128)(2,1)S(1)}, bf16[192,768]{1,0:T(8,128)(2,1)S(1)}, u32[]{:S(2)}, u32[]{:S(2)}) collective-permute-start(bf16[192,768]{1,0:T(8,128)(2,1)S(1)} %collective-permute-done.25.refs_5_), channel_id=1, source_target_pairs={{0,2},{2,0},{4,6},{6,4},{8,10},{10,8},{12,14},{14,12},{16,18},{18,... | collective-permute-start | bytes 884744 | tf_op jit(solution)/shard_map/ppermute | solution.py:139
  52.3 20.7 %collective-permute-start.33 = (bf16[48,1536]{1,0:T(8,128)(2,1)S(1)}, bf16[48,1536]{1,0:T(8,128)(2,1)S(1)}, u32[]{:S(2)}, u32[]{:S(2)}) collective-permute-start(bf16[48,1536]{1,0:T(8,128)(2,1)S(1)} %copy-done.49), channel_id=1, source_target_pairs={{0,16},{2,18},{4,20},{6,22},{8,24},{10,26},{12,28},{14,30},{16,0},... | collective-permute-start | bytes 442376 | tf_op jit(solution)/shard_map/ppermute | solution.py:143
  56.0 19.5 %collective-permute-start.34 = (bf16[48,1536]{1,0:T(8,128)(2,1)S(1)}, bf16[48,1536]{1,0:T(8,128)(2,1)S(1)}, u32[]{:S(2)}, u32[]{:S(2)}) collective-permute-start(bf16[48,1536]{1,0:T(8,128)(2,1)S(1)} %copy-done.49), channel_id=1, source_target_pairs={{0,24},{2,26},{4,28},{6,30},{8,0},{10,2},{12,4},{14,6},{16,8},{18,... | collective-permute-start | bytes 442376 | tf_op jit(solution)/shard_map/ppermute | solution.py:143
  60.6 10.6 %collective-permute-start.29 = (bf16[64,768]{1,0:T(8,128)(2,1)S(1)}, bf16[64,768]{1,0:T(8,128)(2,1)S(1)}, u32[]{:S(2)}, u32[]{:S(2)}) collective-permute-start(bf16[64,768]{1,0:T(8,128)(2,1)S(1)} %copy-done.21), channel_id=1, source_target_pairs={{0,1},{1,0},{2,3},{3,2},{4,5},{5,4},{6,7},{7,6},{8,9},{9,8},{10,11... | collective-permute-start | bytes 294920 | tf_op jit(solution)/shard_map/ppermute | solution.py:184
  62.7 10.9 %collective-permute-start.3 = (bf16[192,768]{1,0:T(8,128)(2,1)S(1)}, bf16[192,768]{1,0:T(8,128)(2,1)S(1)}, u32[]{:S(2)}, u32[]{:S(2)}) collective-permute-start(bf16[192,768]{1,0:T(8,128)(2,1)S(1)} %get-tuple-element.166.refs_0_), channel_id=1, source_target_pairs={{0,2},{2,0},{4,6},{6,4},{8,10},{10,8},{12,14},{14,12},{16,18},{18,... | collective-permute-start | bytes 884744 | tf_op jit(solution)/shard_map/ppermute | solution.py:139
  63.1 12.0 %collective-permute-start.6 = (bf16[192,768]{1,0:T(8,128)(2,1)S(1)}, bf16[192,768]{1,0:T(8,128)(2,1)S(1)}, u32[]{:S(2)}, u32[]{:S(2)}) collective-permute-start(bf16[192,768]{1,0:T(8,128)(2,1)S(1)} %get-tuple-element.165.refs_1_), channel_id=1, source_target_pairs={{0,4},{2,6},{4,0},{6,2},{8,12},{10,14},{12,8},{14,10},{16,20},{18,... | collective-permute-start | bytes 884744 | tf_op jit(solution)/shard_map/ppermute | solution.py:139
  73.6 14.2 %collective-permute-start.7 = (bf16[192,768]{1,0:T(8,128)(2,1)S(1)}, bf16[192,768]{1,0:T(8,128)(2,1)S(1)}, u32[]{:S(2)}, u32[]{:S(2)}) collective-permute-start(bf16[192,768]{1,0:T(8,128)(2,1)S(1)} %collective-permute-done.3.refs_2_), channel_id=1, source_target_pairs={{0,4},{2,6},{4,0},{6,2},{8,12},{10,14},{12,8},{14,10},{16,20},{18,... | collective-permute-start | bytes 884744 | tf_op jit(solution)/shard_map/ppermute | solution.py:139
  75.1 13.2 %collective-permute-start.8 = (bf16[192,768]{1,0:T(8,128)(2,1)S(1)}, bf16[192,768]{1,0:T(8,128)(2,1)S(1)}, u32[]{:S(2)}, u32[]{:S(2)}) collective-permute-start(bf16[192,768]{1,0:T(8,128)(2,1)S(1)} %collective-permute-done.6.refs_5_), channel_id=1, source_target_pairs={{0,2},{2,0},{4,6},{6,4},{8,10},{10,8},{12,14},{14,12},{16,18},{18,... | collective-permute-start | bytes 884744 | tf_op jit(solution)/shard_map/ppermute | solution.py:139
  75.4 14.5 %collective-permute-start.28 = (bf16[256,768]{1,0:T(8,128)(2,1)}, bf16[256,768]{1,0:T(8,128)(2,1)S(1)}, u32[]{:S(2)}, u32[]{:S(2)}) collective-permute-start(bf16[256,768]{1,0:T(8,128)(2,1)} %get-tuple-element.82.refs_10_), channel_id=1, source_target_pairs={{0,1},{1,0},{2,3},{3,2},{4,5},{5,4},{6,7},{7,6},{8,9},{9,8},{10,11... | collective-permute-start | bytes 1179656 | tf_op jit(solution)/shard_map/ppermute | solution.py:184
  81.3 15.6 %collective-permute-start.31 = (bf16[128,768]{1,0:T(8,128)(2,1)S(1)}, bf16[128,768]{1,0:T(8,128)(2,1)S(1)}, u32[]{:S(2)}, u32[]{:S(2)}) collective-permute-start(bf16[128,768]{1,0:T(8,128)(2,1)S(1)} %copy-done.74), channel_id=1, source_target_pairs={{0,1},{1,0},{2,3},{3,2},{4,5},{5,4},{6,7},{7,6},{8,9},{9,8},{10,11... | collective-permute-start | bytes 589832 | tf_op jit(solution)/shard_map/ppermute | solution.py:184
  83.0 17.1 %collective-permute-start.15 = (bf16[192,768]{1,0:T(8,128)(2,1)S(1)}, bf16[192,768]{1,0:T(8,128)(2,1)S(1)}, u32[]{:S(2)}, u32[]{:S(2)}) collective-permute-start(bf16[192,768]{1,0:T(8,128)(2,1)S(1)} %get-tuple-element.163.refs_1_), channel_id=1, source_target_pairs={{0,4},{2,6},{4,0},{6,2},{8,12},{10,14},{12,8},{14,10},{16,20},{18,... | collective-permute-start | bytes 884744 | tf_op jit(solution)/shard_map/ppermute | solution.py:139
  87.8 13.4 %collective-permute-start.13 = (bf16[192,768]{1,0:T(8,128)(2,1)S(1)}, bf16[192,768]{1,0:T(8,128)(2,1)S(1)}, u32[]{:S(2)}, u32[]{:S(2)}) collective-permute-start(bf16[192,768]{1,0:T(8,128)(2,1)S(1)} %get-tuple-element.163.refs_1_), channel_id=1, source_target_pairs={{0,2},{2,0},{4,6},{6,4},{8,10},{10,8},{12,14},{14,12},{16,18},{18,... | collective-permute-start | bytes 884744 | tf_op jit(solution)/shard_map/ppermute | solution.py:139
  89.9 12.2 %collective-permute-start.14 = (bf16[192,768]{1,0:T(8,128)(2,1)S(1)}, bf16[192,768]{1,0:T(8,128)(2,1)S(1)}, u32[]{:S(2)}, u32[]{:S(2)}) collective-permute-start(bf16[192,768]{1,0:T(8,128)(2,1)S(1)} %get-tuple-element.164.refs_0_), channel_id=1, source_target_pairs={{0,4},{2,6},{4,0},{6,2},{8,12},{10,14},{12,8},{14,10},{16,20},{18,... | collective-permute-start | bytes 884744 | tf_op jit(solution)/shard_map/ppermute | solution.py:139
  96.9 21.5 %collective-permute-start.30 = (bf16[256,768]{1,0:T(8,128)(2,1)}, bf16[256,768]{1,0:T(8,128)(2,1)S(1)}, u32[]{:S(2)}, u32[]{:S(2)}) collective-permute-start(bf16[256,768]{1,0:T(8,128)(2,1)} %get-tuple-element.84.refs_9_), channel_id=1, source_target_pairs={{0,1},{1,0},{2,3},{3,2},{4,5},{5,4},{6,7},{7,6},{8,9},{9,8},{10,11... | collective-permute-start | bytes 1179656 | tf_op jit(solution)/shard_map/ppermute | solution.py:184
  101.3 15.1 %collective-permute-start.16 = (bf16[192,768]{1,0:T(8,128)(2,1)S(1)}, bf16[192,768]{1,0:T(8,128)(2,1)S(1)}, u32[]{:S(2)}, u32[]{:S(2)}) collective-permute-start(bf16[192,768]{1,0:T(8,128)(2,1)S(1)} %collective-permute-done.12.refs_2_), channel_id=1, source_target_pairs={{0,4},{2,6},{4,0},{6,2},{8,12},{10,14},{12,8},{14,10},{16,20},{18,... | collective-permute-start | bytes 884744 | tf_op jit(solution)/shard_map/ppermute | solution.py:139
  102.1 15.4 %collective-permute-start.17 = (bf16[192,768]{1,0:T(8,128)(2,1)S(1)}, bf16[192,768]{1,0:T(8,128)(2,1)S(1)}, u32[]{:S(2)}, u32[]{:S(2)}) collective-permute-start(bf16[192,768]{1,0:T(8,128)(2,1)S(1)} %collective-permute-done.15.refs_5_), channel_id=1, source_target_pairs={{0,2},{2,0},{4,6},{6,4},{8,10},{10,8},{12,14},{14,12},{16,18},{18,... | collective-permute-start | bytes 884744 | tf_op jit(solution)/shard_map/ppermute | solution.py:139
  108.3 23.0 %collective-permute-start.36 = (bf16[192,768]{1,0:T(8,128)(2,1)S(1)}, bf16[192,768]{1,0:T(8,128)(2,1)S(1)}, u32[]{:S(2)}, u32[]{:S(2)}) collective-permute-start(bf16[192,768]{1,0:T(8,128)(2,1)S(1)} %get-tuple-element.159.refs_1_), channel_id=1, source_target_pairs={{0,2},{2,0},{4,6},{6,4},{8,10},{10,8},{12,14},{14,12},{16,18},{18,... | collective-permute-start | bytes 884744 | tf_op jit(solution)/shard_map/ppermute | solution.py:139
  110.0 21.6 %collective-permute-start.37 = (bf16[192,768]{1,0:T(8,128)(2,1)S(1)}, bf16[192,768]{1,0:T(8,128)(2,1)S(1)}, u32[]{:S(2)}, u32[]{:S(2)}) collective-permute-start(bf16[192,768]{1,0:T(8,128)(2,1)S(1)} %get-tuple-element.160.refs_0_), channel_id=1, source_target_pairs={{0,4},{2,6},{4,0},{6,2},{8,12},{10,14},{12,8},{14,10},{16,20},{18,... | collective-permute-start | bytes 884744 | tf_op jit(solution)/shard_map/ppermute | solution.py:139
  116.4 16.1 %collective-permute-start.39 = (bf16[192,768]{1,0:T(8,128)(2,1)S(1)}, bf16[192,768]{1,0:T(8,128)(2,1)S(1)}, u32[]{:S(2)}, u32[]{:S(2)}) collective-permute-start(bf16[192,768]{1,0:T(8,128)(2,1)S(1)} %collective-permute-done.35.refs_2_), channel_id=1, source_target_pairs={{0,4},{2,6},{4,0},{6,2},{8,12},{10,14},{12,8},{14,10},{16,20},{18,... | collective-permute-start | bytes 884744 | tf_op jit(solution)/shard_map/ppermute | solution.py:139
  117.5 16.1 %collective-permute-start.40 = (bf16[192,768]{1,0:T(8,128)(2,1)S(1)}, bf16[192,768]{1,0:T(8,128)(2,1)S(1)}, u32[]{:S(2)}, u32[]{:S(2)}) collective-permute-start(bf16[192,768]{1,0:T(8,128)(2,1)S(1)} %collective-permute-done.38.refs_5_), channel_id=1, source_target_pairs={{0,2},{2,0},{4,6},{6,4},{8,10},{10,8},{12,14},{14,12},{16,18},{18,... | collective-permute-start | bytes 884744 | tf_op jit(solution)/shard_map/ppermute | solution.py:139
  128.2 16.1 %collective-permute-start.71 = (bf16[192,768]{1,0:T(8,128)(2,1)}, bf16[192,768]{1,0:T(8,128)(2,1)S(1)}, u32[]{:S(2)}, u32[]{:S(2)}) collective-permute-start(bf16[192,768]{1,0:T(8,128)(2,1)} %get-tuple-element.135), channel_id=1, source_target_pairs={{0,2},{2,0},{4,6},{6,4},{8,10},{10,8},{12,14},{14,12},{16,18},{18,... | collective-permute-start | bytes 884744 | tf_op jit(solution)/shard_map/ppermute | solution.py:139
  131.3 24.8 %collective-permute-start.70 = (bf16[192,768]{1,0:T(8,128)(2,1)}, bf16[192,768]{1,0:T(8,128)(2,1)S(1)}, u32[]{:S(2)}, u32[]{:S(2)}) collective-permute-start(bf16[192,768]{1,0:T(8,128)(2,1)} %get-tuple-element.133), channel_id=1, source_target_pairs={{0,2},{2,0},{4,6},{6,4},{8,10},{10,8},{12,14},{14,12},{16,18},{18,... | collective-permute-start | bytes 884744 | tf_op jit(solution)/shard_map/ppermute | solution.py:139
  131.6 13.1 %collective-permute-start.68 = (bf16[192,768]{1,0:T(8,128)(2,1)}, bf16[192,768]{1,0:T(8,128)(2,1)S(1)}, u32[]{:S(2)}, u32[]{:S(2)}) collective-permute-start(bf16[192,768]{1,0:T(8,128)(2,1)} %get-tuple-element.131), channel_id=1, source_target_pairs={{0,4},{2,6},{4,0},{6,2},{8,12},{10,14},{12,8},{14,10},{16,20},{18,... | collective-permute-start | bytes 884744 | tf_op jit(solution)/shard_map/ppermute | solution.py:139
  132.5 26.2 %collective-permute-start.67 = (bf16[192,768]{1,0:T(8,128)(2,1)}, bf16[192,768]{1,0:T(8,128)(2,1)S(1)}, u32[]{:S(2)}, u32[]{:S(2)}) collective-permute-start(bf16[192,768]{1,0:T(8,128)(2,1)} %get-tuple-element.129), channel_id=1, source_target_pairs={{0,4},{2,6},{4,0},{6,2},{8,12},{10,14},{12,8},{14,10},{16,20},{18,... | collective-permute-start | bytes 884744 | tf_op jit(solution)/shard_map/ppermute | solution.py:139
  144.3 18.6 %collective-permute-start.79 = (bf16[192,768]{1,0:T(8,128)(2,1)}, bf16[192,768]{1,0:T(8,128)(2,1)S(1)}, u32[]{:S(2)}, u32[]{:S(2)}) collective-permute-start(bf16[192,768]{1,0:T(8,128)(2,1)} %get-tuple-element.141), channel_id=1, source_target_pairs={{0,2},{2,0},{4,6},{6,4},{8,10},{10,8},{12,14},{14,12},{16,18},{18,... | collective-permute-start | bytes 884744 | tf_op jit(solution)/shard_map/ppermute | solution.py:139
  144.7 10.3 %collective-permute-start.77 = (bf16[192,768]{1,0:T(8,128)(2,1)}, bf16[192,768]{1,0:T(8,128)(2,1)S(1)}, u32[]{:S(2)}, u32[]{:S(2)}) collective-permute-start(bf16[192,768]{1,0:T(8,128)(2,1)} %get-tuple-element.139), channel_id=1, source_target_pairs={{0,4},{2,6},{4,0},{6,2},{8,12},{10,14},{12,8},{14,10},{16,20},{18,... | collective-permute-start | bytes 884744 | tf_op jit(solution)/shard_map/ppermute | solution.py:139
  156.2 16.9 %collective-permute-start.76 = (bf16[192,768]{1,0:T(8,128)(2,1)S(1)}, bf16[192,768]{1,0:T(8,128)(2,1)S(1)}, u32[]{:S(2)}, u32[]{:S(2)}) collective-permute-start(bf16[192,768]{1,0:T(8,128)(2,1)S(1)} %copy-done.59), channel_id=1, source_target_pairs={{0,4},{2,6},{4,0},{6,2},{8,12},{10,14},{12,8},{14,10},{16,20},{18,... | collective-permute-start | bytes 884744 | tf_op jit(solution)/shard_map/ppermute | solution.py:139
  158.6 34.4 %collective-permute-start.41 = (bf16[512,768]{1,0:T(8,128)(2,1)S(1)}, bf16[512,768]{1,0:T(8,128)(2,1)S(1)}, u32[]{:S(2)}, u32[]{:S(2)}) collective-permute-start(bf16[512,768]{1,0:T(8,128)(2,1)S(1)} %copy-done.12), channel_id=1, source_target_pairs={{0,1},{1,0},{2,3},{3,2},{4,5},{5,4},{6,7},{7,6},{8,9},{9,8},{10,11... | collective-permute-start | bytes 2359304 | tf_op jit(solution)/shard_map/ppermute | solution.py:184
  158.7 10.6 %collective-permute-start.81 = (bf16[192,768]{1,0:T(8,128)(2,1)S(1)}, bf16[192,768]{1,0:T(8,128)(2,1)S(1)}, u32[]{:S(2)}, u32[]{:S(2)}) collective-permute-start(bf16[192,768]{1,0:T(8,128)(2,1)S(1)} %add_convert_fusion.1), channel_id=1, source_target_pairs={{0,4},{2,6},{4,0},{6,2},{8,12},{10,14},{12,8},{14,10},{16,20},{18,... | collective-permute-start | bytes 884744 | tf_op jit(solution)/shard_map/ppermute | solution.py:139
  161.8 14.8 %collective-permute-start.78 = (bf16[192,768]{1,0:T(8,128)(2,1)S(1)}, bf16[192,768]{1,0:T(8,128)(2,1)S(1)}, u32[]{:S(2)}, u32[]{:S(2)}) collective-permute-start(bf16[192,768]{1,0:T(8,128)(2,1)S(1)} %add_convert_fusion.3), channel_id=1, source_target_pairs={{0,2},{2,0},{4,6},{6,4},{8,10},{10,8},{12,14},{14,12},{16,18},{18,... | collective-permute-start | bytes 884744 | tf_op jit(solution)/shard_map/ppermute | solution.py:139
  163.0 13.8 %collective-permute-start.73 = (bf16[48,1536]{1,0:T(8,128)(2,1)S(1)}, bf16[48,1536]{1,0:T(8,128)(2,1)S(1)}, u32[]{:S(2)}, u32[]{:S(2)}) collective-permute-start(bf16[48,1536]{1,0:T(8,128)(2,1)S(1)} %get-tuple-element.147), channel_id=1, source_target_pairs={{0,8},{2,10},{4,12},{6,14},{8,16},{10,18},{12,20},{14,22},{16,24},... | collective-permute-start | bytes 442376 | tf_op jit(solution)/shard_map/ppermute | solution.py:143
  173.1 16.4 %collective-permute-start.75 = (bf16[48,1536]{1,0:T(8,128)(2,1)S(1)}, bf16[48,1536]{1,0:T(8,128)(2,1)S(1)}, u32[]{:S(2)}, u32[]{:S(2)}) collective-permute-start(bf16[48,1536]{1,0:T(8,128)(2,1)S(1)} %get-tuple-element.148), channel_id=1, source_target_pairs={{0,24},{2,26},{4,28},{6,30},{8,0},{10,2},{12,4},{14,6},{16,8},{18,... | collective-permute-start | bytes 442376 | tf_op jit(solution)/shard_map/ppermute | solution.py:143
  176.7 12.9 %collective-permute-start.82 = (bf16[48,1536]{1,0:T(8,128)(2,1)S(1)}, bf16[48,1536]{1,0:T(8,128)(2,1)S(1)}, u32[]{:S(2)}, u32[]{:S(2)}) collective-permute-start(bf16[48,1536]{1,0:T(8,128)(2,1)S(1)} %get-tuple-element.150), channel_id=1, source_target_pairs={{0,8},{2,10},{4,12},{6,14},{8,16},{10,18},{12,20},{14,22},{16,24},... | collective-permute-start | bytes 442376 | tf_op jit(solution)/shard_map/ppermute | solution.py:143
  176.8 16.1 %collective-permute-start.83 = (bf16[48,1536]{1,0:T(8,128)(2,1)S(1)}, bf16[48,1536]{1,0:T(8,128)(2,1)S(1)}, u32[]{:S(2)}, u32[]{:S(2)}) collective-permute-start(bf16[48,1536]{1,0:T(8,128)(2,1)S(1)} %get-tuple-element.152), channel_id=1, source_target_pairs={{0,16},{2,18},{4,20},{6,22},{8,24},{10,26},{12,28},{14,30},{16,0},... | collective-permute-start | bytes 442376 | tf_op jit(solution)/shard_map/ppermute | solution.py:143
  179.3 13.5 %collective-permute-start.84 = (bf16[48,1536]{1,0:T(8,128)(2,1)S(1)}, bf16[48,1536]{1,0:T(8,128)(2,1)S(1)}, u32[]{:S(2)}, u32[]{:S(2)}) collective-permute-start(bf16[48,1536]{1,0:T(8,128)(2,1)S(1)} %get-tuple-element.151), channel_id=1, source_target_pairs={{0,24},{2,26},{4,28},{6,30},{8,0},{10,2},{12,4},{14,6},{16,8},{18,... | collective-permute-start | bytes 442376 | tf_op jit(solution)/shard_map/ppermute | solution.py:143
  206.7 13.6 %collective-permute-start.61 = (bf16[192,768]{1,0:T(8,128)(2,1)S(1)}, bf16[192,768]{1,0:T(8,128)(2,1)S(1)}, u32[]{:S(2)}, u32[]{:S(2)}) collective-permute-start(bf16[192,768]{1,0:T(8,128)(2,1)S(1)} %copy-done.69), channel_id=1, source_target_pairs={{0,2},{2,0},{4,6},{6,4},{8,10},{10,8},{12,14},{14,12},{16,18},{18,... | collective-permute-start | bytes 884744 | tf_op jit(solution)/shard_map/ppermute | solution.py:139
  208.2 15.8 %collective-permute-start.42 = (bf16[384,768]{1,0:T(8,128)(2,1)S(1)}, bf16[384,768]{1,0:T(8,128)(2,1)S(1)}, u32[]{:S(2)}, u32[]{:S(2)}) collective-permute-start(bf16[384,768]{1,0:T(8,128)(2,1)S(1)} %copy-done.14), channel_id=1, source_target_pairs={{0,1},{1,0},{2,3},{3,2},{4,5},{5,4},{6,7},{7,6},{8,9},{9,8},{10,11... | collective-permute-start | bytes 1769480 | tf_op jit(solution)/shard_map/ppermute | solution.py:184
  215.7 21.3 %collective-permute-start.58 = (bf16[192,768]{1,0:T(8,128)(2,1)S(1)}, bf16[192,768]{1,0:T(8,128)(2,1)S(1)}, u32[]{:S(2)}, u32[]{:S(2)}) collective-permute-start(bf16[192,768]{1,0:T(8,128)(2,1)S(1)} %copy-done.58), channel_id=1, source_target_pairs={{0,4},{2,6},{4,0},{6,2},{8,12},{10,14},{12,8},{14,10},{16,20},{18,... | collective-permute-start | bytes 884744 | tf_op jit(solution)/shard_map/ppermute | solution.py:139
  217.1 20.0 %collective-permute-start.60 = (bf16[192,768]{1,0:T(8,128)(2,1)S(1)}, bf16[192,768]{1,0:T(8,128)(2,1)S(1)}, u32[]{:S(2)}, u32[]{:S(2)}) collective-permute-start(bf16[192,768]{1,0:T(8,128)(2,1)S(1)} %add_convert_fusion.11), channel_id=1, source_target_pairs={{0,2},{2,0},{4,6},{6,4},{8,10},{10,8},{12,14},{14,12},{16,18},{18,... | collective-permute-start | bytes 884744 | tf_op jit(solution)/shard_map/ppermute | solution.py:139
  237.2 15.9 %collective-permute-start.50 = (bf16[192,768]{1,0:T(8,128)(2,1)S(1)}, bf16[192,768]{1,0:T(8,128)(2,1)S(1)}, u32[]{:S(2)}, u32[]{:S(2)}) collective-permute-start(bf16[192,768]{1,0:T(8,128)(2,1)S(1)} %copy-done.67), channel_id=1, source_target_pairs={{0,4},{2,6},{4,0},{6,2},{8,12},{10,14},{12,8},{14,10},{16,20},{18,... | collective-permute-start | bytes 884744 | tf_op jit(solution)/shard_map/ppermute | solution.py:139
  238.1 10.4 %collective-permute-start.43 = (bf16[256,768]{1,0:T(8,128)(2,1)S(1)}, bf16[256,768]{1,0:T(8,128)(2,1)S(1)}, u32[]{:S(2)}, u32[]{:S(2)}) collective-permute-start(bf16[256,768]{1,0:T(8,128)(2,1)S(1)} %copy-done.18), channel_id=1, source_target_pairs={{0,1},{1,0},{2,3},{3,2},{4,5},{5,4},{6,7},{7,6},{8,9},{9,8},{10,11... | collective-permute-start | bytes 1179656 | tf_op jit(solution)/shard_map/ppermute | solution.py:184
  238.1 17.9 %collective-permute-start.64 = (bf16[48,1536]{1,0:T(8,128)(2,1)S(1)}, bf16[48,1536]{1,0:T(8,128)(2,1)S(1)}, u32[]{:S(2)}, u32[]{:S(2)}) collective-permute-start(bf16[48,1536]{1,0:T(8,128)(2,1)S(1)} %get-tuple-element.153), channel_id=1, source_target_pairs={{0,8},{2,10},{4,12},{6,14},{8,16},{10,18},{12,20},{14,22},{16,24},... | collective-permute-start | bytes 442376 | tf_op jit(solution)/shard_map/ppermute | solution.py:143
  241.3 16.4 %collective-permute-start.65 = (bf16[48,1536]{1,0:T(8,128)(2,1)S(1)}, bf16[48,1536]{1,0:T(8,128)(2,1)S(1)}, u32[]{:S(2)}, u32[]{:S(2)}) collective-permute-start(bf16[48,1536]{1,0:T(8,128)(2,1)S(1)} %get-tuple-element.155), channel_id=1, source_target_pairs={{0,16},{2,18},{4,20},{6,22},{8,24},{10,26},{12,28},{14,30},{16,0},... | collective-permute-start | bytes 442376 | tf_op jit(solution)/shard_map/ppermute | solution.py:143
  244.7 13.6 %collective-permute-start.66 = (bf16[48,1536]{1,0:T(8,128)(2,1)S(1)}, bf16[48,1536]{1,0:T(8,128)(2,1)S(1)}, u32[]{:S(2)}, u32[]{:S(2)}) collective-permute-start(bf16[48,1536]{1,0:T(8,128)(2,1)S(1)} %get-tuple-element.154), channel_id=1, source_target_pairs={{0,24},{2,26},{4,28},{6,30},{8,0},{10,2},{12,4},{14,6},{16,8},{18,... | collective-permute-start | bytes 442376 | tf_op jit(solution)/shard_map/ppermute | solution.py:143
  248.5 19.9 %collective-permute-start.52 = (bf16[192,768]{1,0:T(8,128)(2,1)S(1)}, bf16[192,768]{1,0:T(8,128)(2,1)S(1)}, u32[]{:S(2)}, u32[]{:S(2)}) collective-permute-start(bf16[192,768]{1,0:T(8,128)(2,1)S(1)} %copy-done.57), channel_id=1, source_target_pairs={{0,2},{2,0},{4,6},{6,4},{8,10},{10,8},{12,14},{14,12},{16,18},{18,... | collective-permute-start | bytes 884744 | tf_op jit(solution)/shard_map/ppermute | solution.py:139
  254.6 16.3 %collective-permute-start.49 = (bf16[192,768]{1,0:T(8,128)(2,1)S(1)}, bf16[192,768]{1,0:T(8,128)(2,1)S(1)}, u32[]{:S(2)}, u32[]{:S(2)}) collective-permute-start(bf16[192,768]{1,0:T(8,128)(2,1)S(1)} %copy-done.56), channel_id=1, source_target_pairs={{0,4},{2,6},{4,0},{6,2},{8,12},{10,14},{12,8},{14,10},{16,20},{18,... | collective-permute-start | bytes 884744 | tf_op jit(solution)/shard_map/ppermute | solution.py:139
  256.1 14.7 %collective-permute-start.54 = (bf16[192,768]{1,0:T(8,128)(2,1)S(1)}, bf16[192,768]{1,0:T(8,128)(2,1)S(1)}, u32[]{:S(2)}, u32[]{:S(2)}) collective-permute-start(bf16[192,768]{1,0:T(8,128)(2,1)S(1)} %add_convert_fusion.13), channel_id=1, source_target_pairs={{0,4},{2,6},{4,0},{6,2},{8,12},{10,14},{12,8},{14,10},{16,20},{18,... | collective-permute-start | bytes 884744 | tf_op jit(solution)/shard_map/ppermute | solution.py:139
  257.6 13.3 %collective-permute-start.51 = (bf16[192,768]{1,0:T(8,128)(2,1)S(1)}, bf16[192,768]{1,0:T(8,128)(2,1)S(1)}, u32[]{:S(2)}, u32[]{:S(2)}) collective-permute-start(bf16[192,768]{1,0:T(8,128)(2,1)S(1)} %add_convert_fusion.15), channel_id=1, source_target_pairs={{0,2},{2,0},{4,6},{6,4},{8,10},{10,8},{12,14},{14,12},{16,18},{18,... | collective-permute-start | bytes 884744 | tf_op jit(solution)/shard_map/ppermute | solution.py:139
  271.1 14.8 %collective-permute-start.55 = (bf16[48,1536]{1,0:T(8,128)(2,1)S(1)}, bf16[48,1536]{1,0:T(8,128)(2,1)S(1)}, u32[]{:S(2)}, u32[]{:S(2)}) collective-permute-start(bf16[48,1536]{1,0:T(8,128)(2,1)S(1)} %get-tuple-element.156), channel_id=1, source_target_pairs={{0,8},{2,10},{4,12},{6,14},{8,16},{10,18},{12,20},{14,22},{16,24},... | collective-permute-start | bytes 442376 | tf_op jit(solution)/shard_map/ppermute | solution.py:143
  271.2 14.7 %collective-permute-start.56 = (bf16[48,1536]{1,0:T(8,128)(2,1)S(1)}, bf16[48,1536]{1,0:T(8,128)(2,1)S(1)}, u32[]{:S(2)}, u32[]{:S(2)}) collective-permute-start(bf16[48,1536]{1,0:T(8,128)(2,1)S(1)} %get-tuple-element.158), channel_id=1, source_target_pairs={{0,16},{2,18},{4,20},{6,22},{8,24},{10,26},{12,28},{14,30},{16,0},... | collective-permute-start | bytes 442376 | tf_op jit(solution)/shard_map/ppermute | solution.py:143
  271.5 14.4 %collective-permute-start.57 = (bf16[48,1536]{1,0:T(8,128)(2,1)S(1)}, bf16[48,1536]{1,0:T(8,128)(2,1)S(1)}, u32[]{:S(2)}, u32[]{:S(2)}) collective-permute-start(bf16[48,1536]{1,0:T(8,128)(2,1)S(1)} %get-tuple-element.157), channel_id=1, source_target_pairs={{0,24},{2,26},{4,28},{6,30},{8,0},{10,2},{12,4},{14,6},{16,8},{18,... | collective-permute-start | bytes 442376 | tf_op jit(solution)/shard_map/ppermute | solution.py:143
  (97 other events, 1130.6 us)
